TPU v7x, 32 devices: a whole 2x2x4 slice. The times are simulated.
32 devices in a mesh: groups: 2 (over y), dp: 16 (over z, x, core).
Axes of the slice: x: 2, y: 2, z: 4, core: 2. Of those that a mesh axis runs over, the one named last changes fastest.
Arguments:
- tokens: bfloat16 [64, 8192], P(('groups', 'dp')), parts along dimension 0, may hold values from -6 to 6
- cotangent: bfloat16 [64, 8192], P(('groups', 'dp')), parts along dimension 0, may hold values from -6 to 6
- gate_weight: bfloat16 [8192, 16384], P(None, 'dp'), may hold values from -0.0625 to 0.0625
- up_weight: bfloat16 [8192, 16384], P(None, 'dp'), may hold values from -0.0625 to 0.0625
- down_weight: bfloat16 [16384, 8192], P('dp'), may hold values from -0.046875 to 0.046875
- kept_blocks: int32 [6, 128, 4], P('groups', 'dp'), parts along dimension 0, may hold values from 0 to 63, as said below
- kept_counts: int32 [6, 128], P('groups', 'dp'), parts along dimension 0, may hold values from 1 to 4, as said below
- sparse_delta: float32 [6, 128, 4, 128, 128], P('groups', 'dp'), parts along dimension 0, may hold values from -0.3125 to 0.3125
- first_moment: float32 [6, 128, 4, 128, 128], P('groups', 'dp'), parts along dimension 0, may hold values from -6 to 6
- second_moment: float32 [6, 128, 4, 128, 128], P('groups', 'dp'), parts along dimension 0, may hold values from 1 to 64
Outputs:
- input_grad: bfloat16 [64, 8192], P(('groups', 'dp')), parts along dimension 0
- new_delta: float32 [6, 128, 4, 128, 128], P('groups', 'dp'), parts along dimension 0
- new_first: float32 [6, 128, 4, 128, 128], P('groups', 'dp'), parts along dimension 0
- new_second: float32 [6, 128, 4, 128, 128], P('groups', 'dp'), parts along dimension 0
There are 2 independent parts, one for each index of `groups`. A program takes and returns all parts, laid end to end along the dimension named above; an argument that names none is the same for every part. Nothing has to cross between parts.
Inputs may be any that keep to these rules, and one draw needn't show every extreme that they name: `kept_blocks`: within a tile the 4 positions are distinct, from 0 to 63; slots at or beyond the tile's count are ignored. `kept_counts`: some tile of every matrix has all 4 slots live.
All inputs are finite; a program needn't handle non-finite values.
Results may differ from a plain program's by a relative error of at most 0.0054.
Values may be sent and summed in bfloat16 or wider, within the bound.
No kernel may reach another device: no remote copies, remote signals or barrier semaphores. Data moves between devices by JAX's collectives and lax.ppermute only.
A program may use at most 320 MiB of HBM per device.

v0:
```python
import functools

import jax
import jax.numpy as jnp
from jax import lax
from jax.experimental import pallas as pl
from jax.experimental.pallas import tpu as pltpu
from jax.sharding import PartitionSpec as P

BF16 = jnp.bfloat16
F32 = jnp.float32
MIB = 1 << 20
VMEM_SPEC = pl.BlockSpec(memory_space=pltpu.VMEM)
SMEM_SPEC = pl.BlockSpec(memory_space=pltpu.SMEM)
HBM_SPEC = pl.BlockSpec(memory_space=pltpu.HBM)


def dot_rows(left, right):
    return lax.dot_general(left, right, (((1,), (1,)), ((), ())), preferred_element_type=F32)


def dot_cols(left, right):
    return lax.dot_general(left, right, (((0,), (0,)), ((), ())), preferred_element_type=F32)


def chunk(i, size):
    return pl.ds(pl.multiple_of(i * size, size), size)


def params(limit):
    return pltpu.CompilerParams(vmem_limit_bytes=limit)


def add_block(ref, rows, cols, block):
    ref[rows, cols] = (ref[rows, cols].astype(F32) + block).astype(BF16)


def add_column_blocks(which, kept, counts, held, ref, first, size):
    tiles, slots, side = held.shape[1:4]
    for t in range(tiles):
        for k in range(slots):
            row = kept[which, t, k] * side

            @pl.when((k < counts[which, t]) & (row >= first) & (row < first + size))
            def _():
                rows = pl.ds(pl.multiple_of(row, side), side)
                add_block(ref, rows, slice(t * side, (t + 1) * side), held[which, t, k])


def side_by_side(array, kept, which, t, side, slots):
    return jnp.concatenate([array[:, chunk(kept[which, t, k], side)] for k in range(slots)], axis=1)


def layer_kernel(
    wide, step, kept, counts, tokens, cotangent, gate_weight, up_weight, down_weight, delta, first, second,
    keep, send, new_delta, new_first, new_second,
    gate_eff, up_eff, held, moments, ring, gate, up, hidden, gate_grad, up_grad,
    held_sems, in_sems, out_sems, ring_sems, part_sems,
):
    width, units = gate_eff.shape
    tiles, slots, side = held.shape[1:4]
    ahead = moments.shape[0] - 1
    half = keep.shape[0]
    depth, height, span = ring.shape
    across = width // span
    chunks = (units // height) * across

    def down_copy(c):
        source = down_weight.at[chunk(c // across, height), chunk(c % across, span)]
        return pltpu.make_async_copy(source, ring.at[c % depth], ring_sems.at[c % depth])

    def read_delta(which):
        return pltpu.make_async_copy(delta.at[which], held.at[which], held_sems.at[which])

    def read(a, t):
        slot = t % (ahead + 1)
        return pltpu.make_async_copy((first, second)[a].at[:, t], moments.at[slot, a], in_sems.at[slot, a])

    def write_delta(t):
        return pltpu.make_async_copy(held.at[:, t], new_delta.at[:, t], out_sems.at[2, t])

    def write(a, t):
        out = (new_first, new_second)[a]
        return pltpu.make_async_copy(moments.at[t % (ahead + 1), a], out.at[:, t], out_sems.at[a, t])

    parts = width // wide

    def part_copy(which, p):
        weight, out = ((gate_weight, gate_eff), (up_weight, up_eff))[which]
        rows = chunk(p, wide)
        return pltpu.make_async_copy(weight.at[rows], out.at[rows], part_sems.at[which, p])

    def forward(which, out, p, carry):
        part_copy(which, p).wait()
        eff = (gate_eff, up_eff)[which]

        @pl.when(p == 0)
        def _():
            read_delta(which).wait()
            out[...] = jnp.zeros_like(out)

        add_column_blocks(which, kept, counts, held, eff, p * wide, wide)
        part = chunk(p, wide)
        out[...] += jnp.dot(tokens[:, part], eff[part, :], preferred_element_type=F32)
        return carry

    read_delta(0).start()
    for p in range(parts):
        part_copy(0, p).start()
    read_delta(1).start()
    for p in range(parts):
        part_copy(1, p).start()
    read_delta(2).start()
    for c in range(min(depth, chunks)):
        down_copy(c).start()
    lax.fori_loop(0, parts, functools.partial(forward, 0, gate), 0)
    for t in range(min(ahead, tiles)):
        for a in range(2):
            read(a, t).start()
    lax.fori_loop(0, parts, functools.partial(forward, 1, up), 0)
    read_delta(2).wait()

    def backward(r, carry):
        hidden_grad = jnp.zeros((2 * half, height), F32)
        for q in range(across):
            c = r * across + q
            down_copy(c).wait()
            slot = ring.at[c % depth]
            for i in range(height // side):
                t = r * (height // side) + i
                for k in range(slots):
                    col = kept[2, t, k] * side - q * span

                    @pl.when((k < counts[2, t]) & (col >= 0) & (col < span))
                    def _():
                        cols = pl.ds(pl.multiple_of(col, side), side)
                        add_block(slot, slice(i * side, (i + 1) * side), cols, held[2, t, k])

            hidden_grad += dot_rows(cotangent[:, q * span : (q + 1) * span], slot[...])

            @pl.when(c + depth < chunks)
            def _():
                down_copy(c + depth).start()

        own = chunk(r, height)
        g, u = gate[:, own], up[:, own]
        sigma = jax.nn.sigmoid(g)
        silu = g * sigma
        hidden[:, own] = (silu * u).astype(BF16)
        gate_grad[:, own] = (hidden_grad * u * sigma * (1.0 + g * (1.0 - sigma))).astype(BF16)
        up_grad[:, own] = (hidden_grad * silu).astype(BF16)
        return carry

    lax.fori_loop(0, units // height, backward, 0)

    def input_part(i):
        part = chunk(i, step)
        both = dot_rows(gate_grad[...], gate_eff[part, :]) + dot_rows(up_grad[...], up_eff[part, :])
        keep[:, part] = both[:half]
        send[:, part] = both[half:].astype(BF16)

    def adam(t):
        own = chunk(t, side)
        slot = t % (ahead + 1)
        for a in range(2):
            read(a, t).wait()
        for which in range(3):
            if which == 2:
                grads = dot_cols(hidden[:, own], side_by_side(cotangent, kept, 2, t, side, slots))
            else:
                right = (gate_grad, up_grad)[which]
                grads = dot_cols(side_by_side(tokens, kept, which, t, side, slots), right[:, own])
            for k in range(slots):
                live = k < counts[which, t]
                part = slice(k * side, (k + 1) * side)
                grad = grads[:, part] if which == 2 else grads[part]
                m1 = 0.9 * moments[slot, 0, which, k] + 0.1 * grad
                m2 = 0.999 * moments[slot, 1, which, k] + 0.001 * grad * grad
                value = held[which, t, k] - 0.01 * m1 / (jnp.sqrt(m2) + 1e-08)
                held[which, t, k] = jnp.where(live, value, 0.0)
                moments[slot, 0, which, k] = jnp.where(live, m1, 0.0)
                moments[slot, 1, which, k] = jnp.where(live, m2, 0.0)
        write_delta(t).start()
        for a in range(2):
            write(a, t).start()

        @pl.when(t + ahead < tiles)
        def _():
            @pl.when(t >= 1)
            def _():
                for a in range(2):
                    write(a, t - 1).wait()

            for a in range(2):
                read(a, t + ahead).start()

    steps = width // step

    def last(i, carry):
        if steps == tiles:
            adam(i)
        input_part(i)
        return carry

    lax.fori_loop(0, steps, last, 0)
    if steps != tiles:
        lax.fori_loop(0, tiles, lambda t, carry: (adam(t), carry)[1], 0)
    for t in range(tiles):
        write_delta(t).wait()
    for t in range(max(tiles - ahead - 1, 0), tiles):
        for a in range(2):
            write(a, t).wait()


def layer(kept, counts, tokens, cotangent, gate_weight, up_weight, down_weight, arrays):
    rows, width = tokens.shape
    units = gate_weight.shape[1]
    shape = arrays[0].shape
    tiles, side = shape[1], shape[-1]
    height, span = min(2, tiles) * side, width // 2
    moment = jax.ShapeDtypeStruct(shape, F32)
    return pl.pallas_call(
        functools.partial(layer_kernel, min(width, 2048), min(width, 1024)),
        out_shape=(
            jax.ShapeDtypeStruct((rows // 2, width), F32),
            jax.ShapeDtypeStruct((rows // 2, width), BF16),
            moment,
            moment,
            moment,
        ),
        in_specs=[SMEM_SPEC] * 2 + [VMEM_SPEC] * 2 + [HBM_SPEC] * 6,
        out_specs=(VMEM_SPEC,) * 2 + (HBM_SPEC,) * 3,
        scratch_shapes=[
            pltpu.VMEM((width, units), BF16),
            pltpu.VMEM((width, units), BF16),
            pltpu.VMEM(shape, F32),
            pltpu.VMEM((4, 2, 3, *shape[2:]), F32),
            pltpu.VMEM((3, height, span), BF16),
            pltpu.VMEM((rows, units), F32),
            pltpu.VMEM((rows, units), F32),
            pltpu.VMEM((rows, units), BF16),
            pltpu.VMEM((rows, units), BF16),
            pltpu.VMEM((rows, units), BF16),
            pltpu.SemaphoreType.DMA((3,)),
            pltpu.SemaphoreType.DMA((4, 2)),
            pltpu.SemaphoreType.DMA((3, tiles)),
            pltpu.SemaphoreType.DMA((3,)),
            pltpu.SemaphoreType.DMA((2, width // min(width, 2048))),
        ],
        compiler_params=params(57 * MIB),
        cost_estimate=pl.CostEstimate(
            flops=10 * rows * width * units, bytes_accessed=10 * width * units, transcendentals=0
        ),
        name="layer",
    )(kept, counts, tokens, cotangent, gate_weight, up_weight, down_weight, *arrays)


def exchange(value, distance, size):
    return lax.ppermute(value, "dp", [(i, i ^ distance) for i in range(size)])


def exchange_order(size):
    distances = [1 << bit for bit in range(size.bit_length() - 1)]
    return distances[1:2] + distances[:1:-1] + distances[:1]


def on_device(
    size,
    tokens,
    cotangent,
    gate_weight,
    up_weight,
    down_weight,
    kept_blocks,
    kept_counts,
    sparse_delta,
    first_moment,
    second_moment,
):
    order = exchange_order(size)
    for distance in order:
        tokens = jnp.concatenate([tokens, exchange(tokens, distance, size)], 0)
    for distance in order:
        cotangent = jnp.concatenate([cotangent, exchange(cotangent, distance, size)], 0)
    arrays = (sparse_delta, first_moment, second_moment)
    total, away, *news = layer(
        kept_blocks, kept_counts, tokens, cotangent, gate_weight, up_weight, down_weight, arrays
    )
    for distance in order[::-1]:
        half = total.shape[0] // 2
        if distance != order[-1]:
            total, away = total[:half], total[half:].astype(BF16)
        total = total + exchange(away, distance, size).astype(F32)
    return (total.astype(BF16), *news)


def solution(mesh):
    rows = P(("groups", "dp"), None)
    blocks = P("groups", "dp", None, None, None)
    return jax.shard_map(
        functools.partial(on_device, mesh.shape["dp"]),
        mesh=mesh,
        in_specs=(
            rows,
            rows,
            P(None, "dp"),
            P(None, "dp"),
            P("dp", None),
            P("groups", "dp", None),
            P("groups", "dp"),
            blocks,
            blocks,
            blocks,
        ),
        out_specs=(rows, blocks, blocks, blocks),
        check_vma=False,
    )
```

profile of v0, /device:TPU:0, one launch (start us, length us, event | category | flops | bytes accessed | tf_op | source)
XLA Modules:
  0.0 93.6 jit_solution(14914870437429277032)
XLA Ops:
  0.6 3.0 %collective-permute-start = (bf16[2,8192]{1,0:T(2,128)(2,1)}, bf16[2,8192]{1,0:T(2,128)(2,1)S(1)}, u32[]{:S(2)}, u32[]{:S(2)}) collective-permute-start(bf16[2,8192]{1,0:T(2,128)(2,1)} %param.10), channel_id=1, source_target_pairs={{0,2},{1,3},{2,0},{3,1},{4,6},{5,7},{6,4},{7,5},{8,10},{9,11},{10,... | collective-permute-start | bytes 98312 | tf_op jit(solution)/shard_map/ppermute | solution.py:259
  3.6 0.1 collective-permute-start.4
  3.7 2.0 %collective-permute-done = bf16[2,8192]{1,0:T(2,128)(2,1)S(1)} collective-permute-done((bf16[2,8192]{1,0:T(2,128)(2,1)}, bf16[2,8192]{1,0:T(2,128)(2,1)S(1)}, u32[]{:S(2)}, u32[]{:S(2)}) %collective-permute-start) | collective-permute-done | bytes 32800 | tf_op jit(solution)/shard_map/ppermute | solution.py:259
  5.7 0.8 pad_maximum_fusion.4
  6.6 3.5 %collective-permute-start.1 = (bf16[4,8192]{1,0:T(4,128)(2,1)S(1)}, bf16[4,8192]{1,0:T(4,128)(2,1)S(1)}, u32[]{:S(2)}, u32[]{:S(2)}) collective-permute-start(bf16[4,8192]{1,0:T(4,128)(2,1)S(1)} %pad_maximum_fusion.4), channel_id=1, source_target_pairs={{0,8},{1,9},{2,10},{3,11},{4,12},{5,13},{6,14},{7,15},{8,0},{9,1},... | collective-permute-start | bytes 196616 | tf_op jit(solution)/shard_map/ppermute | solution.py:259
  10.0 0.0 collective-permute-done.4
  10.0 0.8 pad_maximum_fusion.5
  10.9 0.4 collective-permute-start.5
  11.2 1.0 %collective-permute-done.1 = bf16[4,8192]{1,0:T(4,128)(2,1)S(1)} collective-permute-done((bf16[4,8192]{1,0:T(4,128)(2,1)S(1)}, bf16[4,8192]{1,0:T(4,128)(2,1)S(1)}, u32[]{:S(2)}, u32[]{:S(2)}) %collective-permute-start.1) | collective-permute-done | bytes 65568 | tf_op jit(solution)/shard_map/ppermute | solution.py:259
  12.3 0.9 pad_maximum_fusion.2
  13.1 3.1 %collective-permute-start.2 = (bf16[8,8192]{1,0:T(8,128)(2,1)S(1)}, bf16[8,8192]{1,0:T(8,128)(2,1)S(1)}, u32[]{:S(2)}, u32[]{:S(2)}) collective-permute-start(bf16[8,8192]{1,0:T(8,128)(2,1)S(1)} %pad_maximum_fusion.2), channel_id=1, source_target_pairs={{0,4},{1,5},{2,6},{3,7},{4,0},{5,1},{6,2},{7,3},{8,12},{9,13},{10,... | collective-permute-start | bytes 393224 | tf_op jit(solution)/shard_map/ppermute | solution.py:259
  16.2 0.0 collective-permute-done.5
  16.2 0.9 pad_maximum_fusion.3
  17.1 2.2 %collective-permute-start.6 = (bf16[8,8192]{1,0:T(8,128)(2,1)S(1)}, bf16[8,8192]{1,0:T(8,128)(2,1)S(1)}, u32[]{:S(2)}, u32[]{:S(2)}) collective-permute-start(bf16[8,8192]{1,0:T(8,128)(2,1)S(1)} %pad_maximum_fusion.3), channel_id=1, source_target_pairs={{0,4},{1,5},{2,6},{3,7},{4,0},{5,1},{6,2},{7,3},{8,12},{9,13},{10,... | collective-permute-start | bytes 393224 | tf_op jit(solution)/shard_map/ppermute | solution.py:259
  19.2 1.0 %collective-permute-done.2 = bf16[8,8192]{1,0:T(8,128)(2,1)S(1)} collective-permute-done((bf16[8,8192]{1,0:T(8,128)(2,1)S(1)}, bf16[8,8192]{1,0:T(8,128)(2,1)S(1)}, u32[]{:S(2)}, u32[]{:S(2)}) %collective-permute-start.2) | collective-permute-done | bytes 131104 | tf_op jit(solution)/shard_map/ppermute | solution.py:259
  20.3 0.9 pad_maximum_fusion
  21.2 0.1 collective-permute-start.3
  21.3 0.9 collective-permute-done.6
  22.2 0.9 pad_maximum_fusion.1
  23.1 0.1 collective-permute-start.7
  23.2 1.4 %copy.14.kept = s32[3,8,4]{2,1,0:T(8,128)} copy(s32[3,8,4]{1,2,0:T(4,128)} %param.15) | data formatting | bytes 768 | tf_op args[5]
  24.6 0.0 collective-permute-done.3
  24.6 2.9 %concatenate.33.tokens = bf16[32,8192]{1,0:T(8,128)(2,1)} concatenate(bf16[2,8192]{1,0:T(2,128)(2,1)} %param.10, bf16[2,8192]{1,0:T(2,128)(2,1)S(1)} %collective-permute-done, bf16[4,8192]{1,0:T(4,128)(2,1)S(1)} %collective-permute-done.1, bf16[8,8192]{1,0:T(8,128)(2,1)S(1)} %collective-permute-done.2, bf16[16,8192]{1,0:T(8,128)(2,1)S(1)} %collective-permute-done.3), dimensions={0} | concatenate | bytes 1048576 | tf_op jit(solution)/shard_map/concatenate | solution.py:282
  27.5 0.0 collective-permute-done.7
  27.5 2.9 %concatenate.37.cotangent = bf16[32,8192]{1,0:T(8,128)(2,1)} concatenate(bf16[2,8192]{1,0:T(2,128)(2,1)} %param.11, bf16[2,8192]{1,0:T(2,128)(2,1)S(1)} %collective-permute-done.4, bf16[4,8192]{1,0:T(4,128)(2,1)S(1)} %collective-permute-done.5, bf16[8,8192]{1,0:T(8,128)(2,1)S(1)} %collective-permute-done.6, bf16[16,8192]{1,0:T(8,128)(2,1)S(1)} %collective-permute-done.7), dimensions={0} | concatenate | bytes 1048576 | tf_op jit(solution)/shard_map/concatenate | solution.py:284
  30.5 43.4 %layer.1 = (f32[16,8192]{1,0:T(8,128)}, bf16[16,8192]{1,0:T(8,128)(2,1)}, f32[3,8,4,128,128]{4,3,2,1,0:T(8,128)}, f32[3,8,4,128,128]{4,3,2,1,0:T(8,128)}, f32[3,8,4,128,128]{4,3,2,1,0:T(8,128)}) custom-call(s32[3,8,4]{2,1,0:T(8,128)} %copy.14.kept, s32[3,8]{1,0:T(4,128)} %counts.1, bf16[32,8192]{1,0:T(8,128)(2,1)} %concatenate.33.tokens, ...), custom_call_target="tpu_custom_call" | custom-call | flops 2684354560 | bytes 83886080 | tf_op jit(solution)/shard_map/layer/pallas_call | solution.py:222
  73.9 0.5 collective-permute-start.8
  74.4 1.4 %collective-permute-done.8 = bf16[16,8192]{1,0:T(8,128)(2,1)S(1)} collective-permute-done((bf16[16,8192]{1,0:T(8,128)(2,1)}, bf16[16,8192]{1,0:T(8,128)(2,1)S(1)}, u32[]{:S(2)}, u32[]{:S(2)}) %collective-permute-start.8) | collective-permute-done | bytes 262176 | tf_op jit(solution)/shard_map/ppermute | solution.py:259
  75.8 1.1 %convert_add_fusion = f32[16,8192]{1,0:T(8,128)S(1)} fusion(f32[16,8192]{1,0:T(8,128)} %get-tuple-element.9, bf16[16,8192]{1,0:T(8,128)(2,1)S(1)} %collective-permute-done.8), kind=kLoop, calls=%fused_computation | loop fusion | flops 262144 | bytes 1310720 | tf_op jit(solution)/shard_map/add | solution.py:293
  76.9 2.1 %collective-permute-start.9 = (bf16[8,8192]{1,0:T(8,128)(2,1)S(1)}, bf16[8,8192]{1,0:T(8,128)(2,1)S(1)}, u32[]{:S(2)}, u32[]{:S(2)}) collective-permute-start(bf16[8,8192]{1,0:T(8,128)(2,1)S(1)} %slice.41), channel_id=1, source_target_pairs={{0,4},{1,5},{2,6},{3,7},{4,0},{5,1},{6,2},{7,3},{8,12},{9,13},{10,... | collective-permute-start | bytes 393224 | tf_op jit(solution)/shard_map/ppermute | solution.py:259
  79.1 4.0 %collective-permute-done.9 = bf16[8,8192]{1,0:T(8,128)(2,1)S(1)} collective-permute-done((bf16[8,8192]{1,0:T(8,128)(2,1)S(1)}, bf16[8,8192]{1,0:T(8,128)(2,1)S(1)}, u32[]{:S(2)}, u32[]{:S(2)}) %collective-permute-start.9) | collective-permute-done | bytes 131104 | tf_op jit(solution)/shard_map/ppermute | solution.py:259
  83.2 3.1 %collective-permute-start.10 = (bf16[4,8192]{1,0:T(4,128)(2,1)S(1)}, bf16[4,8192]{1,0:T(4,128)(2,1)S(1)}, u32[]{:S(2)}, u32[]{:S(2)}) collective-permute-start(bf16[4,8192]{1,0:T(4,128)(2,1)S(1)} %slice.42), channel_id=1, source_target_pairs={{0,8},{1,9},{2,10},{3,11},{4,12},{5,13},{6,14},{7,15},{8,0},{9,1},... | collective-permute-start | bytes 196616 | tf_op jit(solution)/shard_map/ppermute | solution.py:259
  86.2 2.6 %collective-permute-done.10 = bf16[4,8192]{1,0:T(4,128)(2,1)S(1)} collective-permute-done((bf16[4,8192]{1,0:T(4,128)(2,1)S(1)}, bf16[4,8192]{1,0:T(4,128)(2,1)S(1)}, u32[]{:S(2)}, u32[]{:S(2)}) %collective-permute-start.10) | collective-permute-done | bytes 65568 | tf_op jit(solution)/shard_map/ppermute | solution.py:259
  88.9 1.8 %collective-permute-start.11 = (bf16[2,8192]{1,0:T(2,128)(2,1)S(1)}, bf16[2,8192]{1,0:T(2,128)(2,1)S(1)}, u32[]{:S(2)}, u32[]{:S(2)}) collective-permute-start(bf16[2,8192]{1,0:T(2,128)(2,1)S(1)} %slice.43), channel_id=1, source_target_pairs={{0,2},{1,3},{2,0},{3,1},{4,6},{5,7},{6,4},{7,5},{8,10},{9,11},{10,... | collective-permute-start | bytes 98312 | tf_op jit(solution)/shard_map/ppermute | solution.py:259
  90.8 2.1 %collective-permute-done.11 = bf16[2,8192]{1,0:T(2,128)(2,1)S(1)} collective-permute-done((bf16[2,8192]{1,0:T(2,128)(2,1)S(1)}, bf16[2,8192]{1,0:T(2,128)(2,1)S(1)}, u32[]{:S(2)}, u32[]{:S(2)}) %collective-permute-start.11) | collective-permute-done | bytes 32800 | tf_op jit(solution)/shard_map/ppermute | solution.py:259
  92.9 0.7 fusion
  (5 shorter events, 0.1 us)
Async XLA Ops:
  0.6 5.1 %collective-permute-start = (bf16[2,8192]{1,0:T(2,128)(2,1)}, bf16[2,8192]{1,0:T(2,128)(2,1)S(1)}, u32[]{:S(2)}, u32[]{:S(2)}) collective-permute-start(bf16[2,8192]{1,0:T(2,128)(2,1)} %param.10), channel_id=1, source_target_pairs={{0,2},{1,3},{2,0},{3,1},{4,6},{5,7},{6,4},{7,5},{8,10},{9,11},{10,... | collective-permute-start | bytes 98312 | tf_op jit(solution)/shard_map/ppermute | solution.py:259
  3.6 6.4 %collective-permute-start.4 = (bf16[2,8192]{1,0:T(2,128)(2,1)}, bf16[2,8192]{1,0:T(2,128)(2,1)S(1)}, u32[]{:S(2)}, u32[]{:S(2)}) collective-permute-start(bf16[2,8192]{1,0:T(2,128)(2,1)} %param.11), channel_id=1, source_target_pairs={{0,2},{1,3},{2,0},{3,1},{4,6},{5,7},{6,4},{7,5},{8,10},{9,11},{10,... | collective-permute-start | bytes 98312 | tf_op jit(solution)/shard_map/ppermute | solution.py:259
  6.6 5.7 %collective-permute-start.1 = (bf16[4,8192]{1,0:T(4,128)(2,1)S(1)}, bf16[4,8192]{1,0:T(4,128)(2,1)S(1)}, u32[]{:S(2)}, u32[]{:S(2)}) collective-permute-start(bf16[4,8192]{1,0:T(4,128)(2,1)S(1)} %pad_maximum_fusion.4), channel_id=1, source_target_pairs={{0,8},{1,9},{2,10},{3,11},{4,12},{5,13},{6,14},{7,15},{8,0},{9,1},... | collective-permute-start | bytes 196616 | tf_op jit(solution)/shard_map/ppermute | solution.py:259
  10.9 5.3 %collective-permute-start.5 = (bf16[4,8192]{1,0:T(4,128)(2,1)S(1)}, bf16[4,8192]{1,0:T(4,128)(2,1)S(1)}, u32[]{:S(2)}, u32[]{:S(2)}) collective-permute-start(bf16[4,8192]{1,0:T(4,128)(2,1)S(1)} %pad_maximum_fusion.5), channel_id=1, source_target_pairs={{0,8},{1,9},{2,10},{3,11},{4,12},{5,13},{6,14},{7,15},{8,0},{9,1},... | collective-permute-start | bytes 196616 | tf_op jit(solution)/shard_map/ppermute | solution.py:259
  13.1 7.1 %collective-permute-start.2 = (bf16[8,8192]{1,0:T(8,128)(2,1)S(1)}, bf16[8,8192]{1,0:T(8,128)(2,1)S(1)}, u32[]{:S(2)}, u32[]{:S(2)}) collective-permute-start(bf16[8,8192]{1,0:T(8,128)(2,1)S(1)} %pad_maximum_fusion.2), channel_id=1, source_target_pairs={{0,4},{1,5},{2,6},{3,7},{4,0},{5,1},{6,2},{7,3},{8,12},{9,13},{10,... | collective-permute-start | bytes 393224 | tf_op jit(solution)/shard_map/ppermute | solution.py:259
  17.1 5.1 %collective-permute-start.6 = (bf16[8,8192]{1,0:T(8,128)(2,1)S(1)}, bf16[8,8192]{1,0:T(8,128)(2,1)S(1)}, u32[]{:S(2)}, u32[]{:S(2)}) collective-permute-start(bf16[8,8192]{1,0:T(8,128)(2,1)S(1)} %pad_maximum_fusion.3), channel_id=1, source_target_pairs={{0,4},{1,5},{2,6},{3,7},{4,0},{5,1},{6,2},{7,3},{8,12},{9,13},{10,... | collective-permute-start | bytes 393224 | tf_op jit(solution)/shard_map/ppermute | solution.py:259
  21.2 3.4 %collective-permute-start.3 = (bf16[16,8192]{1,0:T(8,128)(2,1)S(1)}, bf16[16,8192]{1,0:T(8,128)(2,1)S(1)}, u32[]{:S(2)}, u32[]{:S(2)}) collective-permute-start(bf16[16,8192]{1,0:T(8,128)(2,1)S(1)} %pad_maximum_fusion), channel_id=1, source_target_pairs={{0,1},{1,0},{2,3},{3,2},{4,5},{5,4},{6,7},{7,6},{8,9},{9,8},{10,11... | collective-permute-start | bytes 786440 | tf_op jit(solution)/shard_map/ppermute | solution.py:259
  23.1 4.4 %collective-permute-start.7 = (bf16[16,8192]{1,0:T(8,128)(2,1)S(1)}, bf16[16,8192]{1,0:T(8,128)(2,1)S(1)}, u32[]{:S(2)}, u32[]{:S(2)}) collective-permute-start(bf16[16,8192]{1,0:T(8,128)(2,1)S(1)} %pad_maximum_fusion.1), channel_id=1, source_target_pairs={{0,1},{1,0},{2,3},{3,2},{4,5},{5,4},{6,7},{7,6},{8,9},{9,8},{10,11... | collective-permute-start | bytes 786440 | tf_op jit(solution)/shard_map/ppermute | solution.py:259
  73.9 1.9 %collective-permute-start.8 = (bf16[16,8192]{1,0:T(8,128)(2,1)}, bf16[16,8192]{1,0:T(8,128)(2,1)S(1)}, u32[]{:S(2)}, u32[]{:S(2)}) collective-permute-start(bf16[16,8192]{1,0:T(8,128)(2,1)} %get-tuple-element.10), channel_id=1, source_target_pairs={{0,1},{1,0},{2,3},{3,2},{4,5},{5,4},{6,7},{7,6},{8,9},{9,8},{10,11... | collective-permute-start | bytes 786440 | tf_op jit(solution)/shard_map/ppermute | solution.py:259
  76.9 6.2 %collective-permute-start.9 = (bf16[8,8192]{1,0:T(8,128)(2,1)S(1)}, bf16[8,8192]{1,0:T(8,128)(2,1)S(1)}, u32[]{:S(2)}, u32[]{:S(2)}) collective-permute-start(bf16[8,8192]{1,0:T(8,128)(2,1)S(1)} %slice.41), channel_id=1, source_target_pairs={{0,4},{1,5},{2,6},{3,7},{4,0},{5,1},{6,2},{7,3},{8,12},{9,13},{10,... | collective-permute-start | bytes 393224 | tf_op jit(solution)/shard_map/ppermute | solution.py:259
  83.2 5.7 %collective-permute-start.10 = (bf16[4,8192]{1,0:T(4,128)(2,1)S(1)}, bf16[4,8192]{1,0:T(4,128)(2,1)S(1)}, u32[]{:S(2)}, u32[]{:S(2)}) collective-permute-start(bf16[4,8192]{1,0:T(4,128)(2,1)S(1)} %slice.42), channel_id=1, source_target_pairs={{0,8},{1,9},{2,10},{3,11},{4,12},{5,13},{6,14},{7,15},{8,0},{9,1},... | collective-permute-start | bytes 196616 | tf_op jit(solution)/shard_map/ppermute | solution.py:259
  88.9 4.0 %collective-permute-start.11 = (bf16[2,8192]{1,0:T(2,128)(2,1)S(1)}, bf16[2,8192]{1,0:T(2,128)(2,1)S(1)}, u32[]{:S(2)}, u32[]{:S(2)}) collective-permute-start(bf16[2,8192]{1,0:T(2,128)(2,1)S(1)} %slice.43), channel_id=1, source_target_pairs={{0,2},{1,3},{2,0},{3,1},{4,6},{5,7},{6,4},{7,5},{8,10},{9,11},{10,... | collective-permute-start | bytes 98312 | tf_op jit(solution)/shard_map/ppermute | solution.py:259
where the time goes:
time: 94.4 us; the launch traced here: 93.6 us
  Pallas kernels  43.4 us (46%)
  starting transfers between devices  19.9 us (21%)
  waiting for transfers between devices  15.1 us (16%)
  local copies, waits for them, and re-layouts  7.35 us (8%)
  other arithmetic  7.06 us (7%)
    pallas_call x1, Pallas kernels, layer(): pl.pallas_call(functools.partial(layer_kernel, min(width, 2048), min(widt...  43.4 us
    ppermute x12, starting transfers between devices, exchange(): return lax.ppermute(value, 'dp', [(i, i ^ distance) for i in range(size)])  19.9 us
    ppermute x12, waiting for transfers between devices, exchange(): return lax.ppermute(value, 'dp', [(i, i ^ distance) for i in range(size)])  15.1 us
    concatenate x1, local copies, waits for them, and re-layouts, on_device(): jnp.concatenate([cotangent, exchange(cotangent, distance, size)], 0)  2.95 us
    concatenate x1, local copies, waits for them, and re-layouts, on_device(): tokens = jnp.concatenate([tokens, exchange(tokens, distance, size)], 0)  2.94 us
    concatenate x3, other arithmetic, on_device(): jnp.concatenate([cotangent, exchange(cotangent, distance, size)], 0)  2.63 us
    concatenate x3, other arithmetic, on_device(): tokens = jnp.concatenate([tokens, exchange(tokens, distance, size)], 0)  2.63 us
  transfers between devices with their start and end apart: 12, of which 8 were waited for; matrix products, arithmetic and copies ran while one was open for 10% of the time, Pallas kernels for 0%

commit v1 on v0

v1 whole, which is shorter than its diff:
```python
import functools

import jax
import jax.numpy as jnp
from jax import lax
from jax.experimental import pallas as pl
from jax.experimental.pallas import tpu as pltpu
from jax.sharding import PartitionSpec as P

BF16 = jnp.bfloat16
F32 = jnp.float32
MIB = 1 << 20
VMEM_SPEC = pl.BlockSpec(memory_space=pltpu.VMEM)
SMEM_SPEC = pl.BlockSpec(memory_space=pltpu.SMEM)
HBM_SPEC = pl.BlockSpec(memory_space=pltpu.HBM)


def in_hbm(*arrays):
    return [pltpu.with_memory_space_constraint(array, pltpu.HBM) for array in arrays]


def in_vmem(*arrays):
    return [pltpu.with_memory_space_constraint(array, pltpu.VMEM) for array in arrays]


def dot_rows(left, right):
    return lax.dot_general(left, right, (((1,), (1,)), ((), ())), preferred_element_type=F32)


def dot_cols(left, right):
    return lax.dot_general(left, right, (((0,), (0,)), ((), ())), preferred_element_type=F32)


def chunk(i, size):
    return pl.ds(pl.multiple_of(i * size, size), size)


def params(limit):
    return pltpu.CompilerParams(vmem_limit_bytes=limit)


def cost(flops, moved):
    return pl.CostEstimate(flops=flops, bytes_accessed=moved, transcendentals=0)


def add_block(ref, rows, cols, block):
    ref[rows, cols] = (ref[rows, cols].astype(F32) + block).astype(BF16)


def enter_kernel(count, *refs):
    blocks, targets, sems = refs[count], refs[count + 1 : -1], refs[-1]
    sources = [*refs[:count], *(blocks.at[i] for i in range(blocks.shape[0]))]
    copies = [
        pltpu.make_async_copy(source, target, sems.at[i])
        for i, (source, target) in enumerate(zip(sources, targets))
    ]
    for copy in copies:
        copy.start()
    for copy in copies:
        copy.wait()


def into_vmem(*arrays):
    *whole, blocks = arrays
    shapes = [array.shape for array in whole] + [blocks.shape[1:]] * blocks.shape[0]
    kinds = [array.dtype for array in whole] + [blocks.dtype] * blocks.shape[0]
    return pl.pallas_call(
        functools.partial(enter_kernel, len(whole)),
        out_shape=tuple(pltpu.VMEM(*out) for out in zip(shapes, kinds)),
        in_specs=[HBM_SPEC] * len(arrays),
        scratch_shapes=[pltpu.SemaphoreType.DMA((len(shapes),))],
        compiler_params=params(2 * MIB),
        name="enter",
    )(*in_hbm(*arrays))


def add_column_blocks(which, kept, counts, delta, ref, offset, first, size):
    tiles, slots, side = delta.shape[:3]
    for t in range(tiles):
        for k in range(slots):
            row = kept[which, k, t] * side - offset

            @pl.when((k < counts[which, t]) & (row >= first) & (row < first + size))
            def _():
                rows = pl.ds(pl.multiple_of(row, side), side)
                add_block(ref, rows, slice(t * side, (t + 1) * side), delta[t, k])


def patch_kernel(which, offset, step, kept, counts, delta, weight, out, sems):
    parts = out.shape[0] // step

    def part_copy(p):
        source = weight.at[pl.ds(offset + p * step, step)]
        return pltpu.make_async_copy(source, out.at[pl.ds(p * step, step)], sems.at[p])

    for p in range(parts):
        part_copy(p).start()
    for p in range(parts):
        part_copy(p).wait()
        add_column_blocks(which, kept, counts, delta, out, offset, p * step, step)


def patched(which, offset, height, kept, counts, delta, weight):
    units = weight.shape[1]
    step = height // 2
    return pl.pallas_call(
        functools.partial(patch_kernel, which, offset, step),
        out_shape=pltpu.VMEM((height, units), BF16),
        in_specs=[SMEM_SPEC, SMEM_SPEC, VMEM_SPEC, HBM_SPEC],
        scratch_shapes=[pltpu.SemaphoreType.DMA((height // step,))],
        compiler_params=params(4 * MIB),
        cost_estimate=cost(0, 2 * height * units),
        name="patch",
    )(kept, counts, *in_vmem(delta), *in_hbm(weight))


def moment_copies(which, sources, targets, sems, row=0):
    return [
        pltpu.make_async_copy(source.at[which], target, sems.at[i, row])
        for i, (source, target) in enumerate(zip(sources, targets))
    ]


def moments_kernel(which, first, second, first_out, second_out, sems):
    copies = moment_copies(which, (first, second), (first_out, second_out), sems)
    for copy in copies:
        copy.start()
    for copy in copies:
        copy.wait()


def moments(which, first, second):
    out = pltpu.VMEM(first.shape[1:], F32)
    return pl.pallas_call(
        functools.partial(moments_kernel, which),
        out_shape=(out, out),
        in_specs=[HBM_SPEC] * 2,
        scratch_shapes=[pltpu.SemaphoreType.DMA((2, 1))],
        compiler_params=params(2 * MIB),
        cost_estimate=cost(0, 8 * first[0].size),
        name="moments",
    )(*in_hbm(first, second))


def layer_kernel(
    wide, step, kept, counts, tokens_0, tokens_1, cotangent_0, cotangent_1,
    gate_0, gate_1, up_delta, down_delta, up_weight, down_weight, first, second,
    keep, send, tokens, cotangent, hidden, gate_grad, up_grad, *refs,
):
    moments_out = refs[:-7]
    up_eff, ring, gate, up, ring_sems, part_sems, moment_sems = refs[-7:]
    width, units = up_eff.shape
    tiles, slots, side = up_delta.shape[:3]
    half = keep.shape[0]
    depth, height, span = ring.shape
    across = width // span
    chunks = (units // height) * across

    def down_copy(c):
        source = down_weight.at[chunk(c // across, height), chunk(c % across, span)]
        return pltpu.make_async_copy(source, ring.at[c % depth], ring_sems.at[c % depth])

    lower = width // 2
    parts = width // wide
    flight = 3

    def part_copy(p):
        rows = chunk(p, wide)
        return pltpu.make_async_copy(up_weight.at[rows], up_eff.at[rows], part_sems.at[p])

    def start(j):
        @pl.when(j < parts)
        def _():
            part_copy(j).start()

        @pl.when((j >= parts) & (j < parts + min(depth, chunks)))
        def _():
            down_copy(j - parts).start()

    for j in range(flight):
        start(j)
    for whole, part_0, part_1 in (
        (tokens, tokens_0, tokens_1),
        (cotangent, cotangent_0, cotangent_1),
    ):
        whole[:half] = part_0[...]
        whole[half:] = part_1[...]
    gate[...] = jnp.zeros_like(gate)
    up[...] = jnp.zeros_like(up)

    def product(out, eff, first_part, i):
        left = tokens[:, chunk(first_part + i, wide)]
        out[...] += jnp.dot(left, eff[chunk(i, wide), :], preferred_element_type=F32)

    def forward_gate(eff, first_part, i, carry):
        product(gate, eff, first_part, i)
        return carry

    def forward_up(p, carry):
        part_copy(p).wait()
        start(p + flight)
        add_column_blocks(1, kept, counts, up_delta, up_eff, 0, p * wide, wide)
        product(up, up_eff, 0, p)
        return carry

    lax.fori_loop(0, parts // 2, functools.partial(forward_gate, gate_0, 0), 0)
    lax.fori_loop(0, parts // 2, functools.partial(forward_gate, gate_1, parts // 2), 0)
    lax.fori_loop(0, parts, forward_up, 0)

    def backward(r, carry):
        hidden_grad = jnp.zeros((2 * half, height), F32)
        for q in range(across):
            c = r * across + q
            down_copy(c).wait()
            slot = ring.at[c % depth]
            for i in range(height // side):
                t = r * (height // side) + i
                for k in range(slots):
                    col = kept[2, k, t] * side - q * span

                    @pl.when((k < counts[2, t]) & (col >= 0) & (col < span))
                    def _():
                        cols = pl.ds(pl.multiple_of(col, side), side)
                        add_block(slot, slice(i * side, (i + 1) * side), cols, down_delta[t, k])

            hidden_grad += dot_rows(cotangent[:, q * span : (q + 1) * span], slot[...])

            @pl.when(c + depth < chunks)
            def _():
                down_copy(c + depth).start()

        own = chunk(r, height)
        g, u = gate[:, own], up[:, own]
        sigma = jax.nn.sigmoid(g)
        silu = g * sigma
        hidden[:, own] = (silu * u).astype(BF16)
        gate_grad[:, own] = (hidden_grad * u * sigma * (1.0 + g * (1.0 - sigma))).astype(BF16)
        up_grad[:, own] = (hidden_grad * silu).astype(BF16)
        return carry

    lax.fori_loop(0, units // height, backward, 0)
    copies = []
    for which in range(len(moments_out) // 2):
        targets = moments_out[2 * which : 2 * which + 2]
        copies += moment_copies(which, (first, second), targets, moment_sems, which)
    for copy in copies:
        copy.start()

    def input_part(gate_eff, offset, i, carry):
        cols = chunk(offset // step + i, step)
        both = dot_rows(gate_grad[...], gate_eff[chunk(i, step), :])
        both += dot_rows(up_grad[...], up_eff[cols, :])
        keep[:, cols] = both[:half]
        send[:, cols] = both[half:].astype(BF16)
        return carry

    lax.fori_loop(0, lower // step, functools.partial(input_part, gate_0, 0), 0)
    lax.fori_loop(0, lower // step, functools.partial(input_part, gate_1, lower), 0)
    for copy in copies:
        copy.wait()


def layer(ahead, kept, counts, tokens, cotangent, gate_eff, deltas, up_weight, down_weight, first, second):
    rows, width = 2 * tokens[0].shape[0], tokens[0].shape[1]
    units = gate_eff[0].shape[1]
    shape = first.shape
    tiles, side = shape[1], shape[-1]
    height, span = min(2, tiles) * side, width // 2
    wide, step = width // 4, width // 8
    grad = pltpu.VMEM((rows, units), BF16)
    return pl.pallas_call(
        functools.partial(layer_kernel, wide, step),
        out_shape=(
            pltpu.VMEM((rows // 2, width), F32),
            pltpu.VMEM((rows // 2, width), BF16),
            pltpu.VMEM((rows, width), BF16),
            pltpu.VMEM((rows, width), BF16),
            grad,
            grad,
            grad,
            *(pltpu.VMEM(shape[1:], F32),) * (2 * ahead),
        ),
        in_specs=[SMEM_SPEC] * 2 + [VMEM_SPEC] * 8 + [HBM_SPEC] * 4,
        scratch_shapes=[
            pltpu.VMEM((width, units), BF16),
            pltpu.VMEM((3, height, span), BF16),
            pltpu.VMEM((rows, units), F32),
            pltpu.VMEM((rows, units), F32),
            pltpu.SemaphoreType.DMA((3,)),
            pltpu.SemaphoreType.DMA((width // wide,)),
            pltpu.SemaphoreType.DMA((2, max(ahead, 1))),
        ],
        compiler_params=params(25 * MIB),
        cost_estimate=cost(10 * rows * width * units, 10 * width * units),
        name="layer",
    )(
        kept,
        counts,
        *in_vmem(*tokens, *cotangent, *gate_eff, *deltas[1:]),
        *in_hbm(up_weight, down_weight, first, second),
    )


def adam_kernel(which, kept, counts, left, right, delta, first, second, *refs):
    outs = refs[-5:-2]
    made, sems = refs[-2:]
    tiles, slots, side = delta.shape[:3]

    def write(a, t):
        return pltpu.make_async_copy(made.at[a, t], outs[a].at[which, t], sems.at[a, t])

    def tile(t, carry):
        own = chunk(t, side)
        for k in range(slots):
            block = chunk(kept[which, k, t], side)
            if which == 2:
                grad = dot_cols(left[:, own], right[:, block])
            else:
                grad = dot_cols(left[:, block], right[:, own])
            live = k < counts[which, t]
            m1 = 0.9 * first[t, k] + 0.1 * grad
            m2 = 0.999 * second[t, k] + 0.001 * grad * grad
            value = delta[t, k] - 0.01 * m1 / (jnp.sqrt(m2) + 1e-08)
            for a, new in enumerate((value, m1, m2)):
                made[a, t, k] = jnp.where(live, new, 0.0)
        for a in range(3):
            write(a, t).start()
        return carry

    lax.fori_loop(0, tiles, tile, 0, unroll=min(tiles, 2))
    for t in range(tiles):
        for a in range(3):
            write(a, t).wait()


def adam(which, kept, counts, left, right, delta, moment_pair, done):
    shape = (3, *delta.shape)
    out = pltpu.HBM(shape, F32)
    return pl.pallas_call(
        functools.partial(adam_kernel, which),
        out_shape=(out, out, out),
        in_specs=[SMEM_SPEC] * 2 + [VMEM_SPEC] * 5 + [HBM_SPEC] * len(done),
        out_specs=(HBM_SPEC,) * 3,
        scratch_shapes=[pltpu.VMEM((3, *shape[1:]), F32), pltpu.SemaphoreType.DMA((3, shape[1]))],
        input_output_aliases={7 + i: i for i in range(len(done))},
        compiler_params=params(8 * MIB),
        cost_estimate=cost(0, 12 * delta.size),
        name="adam",
    )(kept, counts, *in_vmem(left, right, delta, *moment_pair), *in_hbm(*done))


def exchange(value, distance, size):
    return lax.ppermute(value, "dp", [(i, i ^ distance) for i in range(size)])


def exchange_order(size):
    distances = [1 << bit for bit in range(size.bit_length() - 1)]
    return distances[1:2] + distances[:1:-1] + distances[:1]


def after(value, *others):
    return lax.optimization_barrier((value, others))[0]


def on_device(
    size,
    tokens,
    cotangent,
    gate_weight,
    up_weight,
    down_weight,
    kept_blocks,
    kept_counts,
    sparse_delta,
    first_moment,
    second_moment,
):
    order = exchange_order(size)
    raw = (tokens, cotangent)
    tokens, cotangent, kept, counts, *deltas = into_vmem(
        tokens, cotangent, kept_blocks.transpose(0, 2, 1), kept_counts, sparse_delta
    )
    half = gate_weight.shape[0] // 2
    pair = (tokens, cotangent)
    gate_eff = []
    for i, distance in enumerate(order):
        got = tuple(exchange(rows, distance, size) for rows in (pair if i else raw))
        if max(len(order) - 3, 0) <= i < len(order) - 1:
            offset = len(gate_eff) * half
            gate_eff.append(patched(0, offset, half, after(kept, *pair), counts, deltas[0], gate_weight))
        if i < len(order) - 1:
            pair = tuple(jnp.concatenate(both, 0) for both in zip(pair, got))
            pair = after(pair, *deltas, *gate_eff[-1:])
    tokens, cotangent = zip(pair, got)
    ahead = 3
    total, away, tokens, cotangent, hidden, gate_grad, up_grad, *fetched = layer(
        ahead, kept, counts, tokens, cotangent, gate_eff, deltas, up_weight, down_weight, first_moment, second_moment
    )
    operands = ((tokens, gate_grad), (tokens, up_grad), (hidden, cotangent))
    news = ()
    for i, distance in enumerate(order[::-1]):
        if i:
            half = total.shape[0] // 2
            total, away = total[:half], total[half:].astype(BF16)
        got = exchange(away, distance, size)
        which = i - (len(order) - 3)
        if which == -1 or (which == 0 and i == 0):
            for late in range(ahead, 3):
                fetched += moments(late, after(first_moment, away), second_moment)
            got = after(got, *fetched)
        if which >= 0:
            pair = fetched[2 * which : 2 * which + 2]
            news = adam(which, after(kept, away), counts, *operands[which], deltas[which], pair, news)
        total = total + got.astype(F32)
        if which >= 0:
            total = after(total, *news)
    return (total.astype(BF16), *news)


def solution(mesh):
    rows = P(("groups", "dp"), None)
    blocks = P("groups", "dp", None, None, None)
    return jax.shard_map(
        functools.partial(on_device, mesh.shape["dp"]),
        mesh=mesh,
        in_specs=(
            rows,
            rows,
            P(None, "dp"),
            P(None, "dp"),
            P("dp", None),
            P("groups", "dp", None),
            P("groups", "dp"),
            blocks,
            blocks,
            blocks,
        ),
        out_specs=(rows, blocks, blocks, blocks),
        check_vma=False,
    )
```

time: 94.4 us -> 73.5 us (0.78)
  waiting for transfers between devices: 15.1 us -> 6.6 us
  Pallas kernels: 43.4 us -> 50.9 us
  local copies, waits for them, and re-layouts: 7.35 us -> 0.11 us
  starting transfers between devices: 19.9 us -> 13.8 us
  other arithmetic: 7.06 us -> 1.11 us
    ppermute x12, waiting for transfers between devices: 15.1 us -> 6.6 us  [exchange(): return lax.ppermute(value, 'dp', [(i, i ^ distance) for i in range(size)])]
    pallas_call x1 -> x7, Pallas kernels: 43.4 us -> 50.9 us  [the longest x1 26.8 us: layer(): pl.pallas_call(functools.partial(layer_kernel, wide, step), out_shape=(pl...]
    ppermute x12, starting transfers between devices: 19.9 us -> 13.8 us  [exchange(): return lax.ppermute(value, 'dp', [(i, i ^ distance) for i in range(size)])]
    concatenate x2 -> x0, local copies, waits for them, and re-layouts: 5.89 us -> none  [the longest x1 2.95 us: on_device(): jnp.concatenate([cotangent, exchange(cotangent, distance, size)], 0)]
    concatenate x6, other arithmetic: 5.26 us -> 0.32 us  [on_device(): pair = tuple((jnp.concatenate(both, 0) for both in zip(pair, got)))]
    unnamed x1 -> x8, local copies, waits for them, and re-layouts: 1.38 us -> 0.03 us
  transfers between devices with their start and end apart: 12 -> 12, of which waited for: 8 -> 7; matrix products, arithmetic and copies ran while one was open for 10% -> 0% of each run, Pallas kernels for 0% -> 33%
where the time goes in v1:
time: 73.5 us; the launch traced here: 73.4 us
  Pallas kernels  50.9 us (69%)
  starting transfers between devices  13.8 us (19%)
  waiting for transfers between devices  6.6 us (9%)
  other arithmetic  1.11 us (2%)
  between operations  0.84 us (1%)
    pallas_call x1, Pallas kernels, layer(): pl.pallas_call(functools.partial(layer_kernel, wide, step), out_shape=(pl...  26.8 us
    ppermute x12, starting transfers between devices, exchange(): return lax.ppermute(value, 'dp', [(i, i ^ distance) for i in range(size)])  13.8 us
    pallas_call x3, Pallas kernels, adam(): pl.pallas_call(functools.partial(adam_kernel, which), out_shape=(out, out...  12.2 us
    pallas_call x2, Pallas kernels, patched(): pl.pallas_call(functools.partial(patch_kernel, which, offset, step), out_...  8.94 us
    ppermute x12, waiting for transfers between devices, exchange(): return lax.ppermute(value, 'dp', [(i, i ^ distance) for i in range(size)])  6.6 us
    pallas_call x1, Pallas kernels, into_vmem(): pl.pallas_call(functools.partial(enter_kernel, len(whole)), out_shape=tup...  2.98 us
  transfers between devices with their start and end apart: 12, of which 7 were waited for; matrix products, arithmetic and copies ran while one was open for 0% of the time, Pallas kernels for 33%

profile of v1, /device:TPU:0, one launch (start us, length us, event | category | flops | bytes accessed | tf_op | source)
XLA Modules:
  0.0 73.4 jit_solution(4974171350328105352)
XLA Ops:
  0.6 3.0 %collective-permute-start = (bf16[2,8192]{1,0:T(2,128)(2,1)}, bf16[2,8192]{1,0:T(2,128)(2,1)S(1)}, u32[]{:S(2)}, u32[]{:S(2)}) collective-permute-start(bf16[2,8192]{1,0:T(2,128)(2,1)} %refs_0_.1), channel_id=1, source_target_pairs={{0,2},{1,3},{2,0},{3,1},{4,6},{5,7},{6,4},{7,5},{8,10},{9,11},{10,... | collective-permute-start | bytes 98312 | tf_op jit(solution)/shard_map/ppermute | solution.py:353
  3.6 0.1 collective-permute-start.1
  3.7 3.0 %enter.1 = (bf16[2,8192]{1,0:T(2,128)(2,1)S(1)}, bf16[2,8192]{1,0:T(2,128)(2,1)S(1)}, s32[3,4,8]{2,1,0:T(4,128)S(1)}, s32[3,8]{1,0:T(4,128)S(1)}, f32[8,4,128,12...) custom-call(bf16[2,8192]{1,0:T(2,128)(2,1)} %refs_0_.1, bf16[2,8192]{1,0:T(2,128)(2,1)} %refs_1_.1, ...), custom_call_target="tpu_custom_call" | custom-call | tf_op jit(solution)/shard_map/enter/pallas_call | solution.py:67
  6.7 0.0 copy-start
  6.7 0.0 copy-start.2
  6.7 0.0 collective-permute-done
  6.7 0.1 pad_maximum_fusion.4
  6.8 0.9 %collective-permute-done.1 = bf16[2,8192]{1,0:T(2,128)(2,1)S(1)} collective-permute-done((bf16[2,8192]{1,0:T(2,128)(2,1)}, bf16[2,8192]{1,0:T(2,128)(2,1)S(1)}, u32[]{:S(2)}, u32[]{:S(2)}) %collective-permute-start.1) | collective-permute-done | bytes 32800 | tf_op jit(solution)/shard_map/ppermute | solution.py:353
  7.8 0.1 pad_maximum_fusion.5
  7.8 2.7 %collective-permute-start.2 = (bf16[4,8192]{1,0:T(4,128)(2,1)S(1)}, bf16[4,8192]{1,0:T(4,128)(2,1)S(1)}, u32[]{:S(2)}, u32[]{:S(2)}) collective-permute-start(bf16[4,8192]{1,0:T(4,128)(2,1)S(1)} %pad_maximum_fusion.4), channel_id=1, source_target_pairs={{0,8},{1,9},{2,10},{3,11},{4,12},{5,13},{6,14},{7,15},{8,0},{9,1},... | collective-permute-start | bytes 196616 | tf_op jit(solution)/shard_map/ppermute | solution.py:353
  10.5 0.3 collective-permute-start.3
  10.8 4.4 %patch.2.gate_0 = bf16[4096,1024]{1,0:T(8,128)(2,1)S(1)} custom-call(s32[3,4,8]{2,1,0:T(4,128)S(1)} %get-tuple-element.85.kept, s32[3,8]{1,0:T(4,128)S(1)} %get-tuple-element.49.counts, f32[8,4,128,128]{3,2,1,0:T(8,128)S(1)} %get-tuple-element.52.delta, bf16[8192,1024]{1,0:T(8,128)(2,1)} %weight.3), custom_call_target="tpu_custom_call" | custom-call | bytes 8388608 | tf_op jit(solution)/shard_map/patch/pallas_call | solution.py:106
  15.3 0.0 collective-permute-done.2
  15.3 0.1 pad_maximum_fusion.2
  15.4 0.5 collective-permute-done.3
  15.9 0.1 pad_maximum_fusion.3
  15.9 1.4 %collective-permute-start.4 = (bf16[8,8192]{1,0:T(8,128)(2,1)S(1)}, bf16[8,8192]{1,0:T(8,128)(2,1)S(1)}, u32[]{:S(2)}, u32[]{:S(2)}) collective-permute-start(bf16[8,8192]{1,0:T(8,128)(2,1)S(1)} %pad_maximum_fusion.2), channel_id=1, source_target_pairs={{0,4},{1,5},{2,6},{3,7},{4,0},{5,1},{6,2},{7,3},{8,12},{9,13},{10,... | collective-permute-start | bytes 393224 | tf_op jit(solution)/shard_map/ppermute | solution.py:353
  17.4 0.7 collective-permute-start.5
  18.0 0.0 copy-done
  18.0 0.0 copy-done.2
  18.0 4.5 %patch.3.gate_1 = bf16[4096,1024]{1,0:T(8,128)(2,1)S(1)} custom-call(s32[3,4,8]{2,1,0:T(4,128)S(1)} %get-tuple-element.85.kept, s32[3,8]{1,0:T(4,128)S(1)} %get-tuple-element.49.counts, f32[8,4,128,128]{3,2,1,0:T(8,128)S(1)} %get-tuple-element.52.delta, bf16[8192,1024]{1,0:T(8,128)(2,1)} %weight.3), custom_call_target="tpu_custom_call" | custom-call | bytes 8388608 | tf_op jit(solution)/shard_map/patch/pallas_call | solution.py:106
  22.6 0.0 collective-permute-done.4
  22.6 1.2 %collective-permute-done.5 = bf16[8,8192]{1,0:T(8,128)(2,1)S(1)} collective-permute-done((bf16[8,8192]{1,0:T(8,128)(2,1)S(1)}, bf16[8,8192]{1,0:T(8,128)(2,1)S(1)}, u32[]{:S(2)}, u32[]{:S(2)}) %collective-permute-start.5) | collective-permute-done | bytes 131104 | tf_op jit(solution)/shard_map/ppermute | solution.py:353
  23.8 0.0 copy-start.1
  23.8 0.0 copy-start.3
  23.8 0.1 collective-permute-start.6
  23.9 0.5 collective-permute-start.7
  24.4 1.0 %collective-permute-done.6.tokens_1 = bf16[16,8192]{1,0:T(8,128)(2,1)S(1)} collective-permute-done((bf16[16,8192]{1,0:T(8,128)(2,1)S(1)}, bf16[16,8192]{1,0:T(8,128)(2,1)S(1)}, u32[]{:S(2)}, u32[]{:S(2)}) %collective-permute-start.6) | collective-permute-done | bytes 262176 | tf_op jit(solution)/shard_map/ppermute | solution.py:353
  25.4 0.4 collective-permute-done.7.cotangent_1
  25.8 26.8 %layer.1 = (f32[16,8192]{1,0:T(8,128)S(1)}, bf16[16,8192]{1,0:T(8,128)(2,1)S(1)}, bf16[32,8192]{1,0:T(8,128)(2,1)S(1)}, bf16[32,8192]{1,0:T(8,128)(2,1)S(1)}, bf...) custom-call(s32[3,4,8]{2,1,0:T(4,128)} %copy-done, ...), custom_call_target="tpu_custom_call" | custom-call | flops 2684354560 | bytes 83886080 | tf_op jit(solution)/shard_map/layer/pallas_call | solution.py:271
  52.6 0.1 collective-permute-start.8
  52.7 1.5 %collective-permute-done.8 = bf16[16,8192]{1,0:T(8,128)(2,1)S(1)} collective-permute-done((bf16[16,8192]{1,0:T(8,128)(2,1)S(1)}, bf16[16,8192]{1,0:T(8,128)(2,1)S(1)}, u32[]{:S(2)}, u32[]{:S(2)}) %collective-permute-start.8) | collective-permute-done | bytes 262176 | tf_op jit(solution)/shard_map/ppermute | solution.py:353
  54.2 0.1 convert_add_fusion
  54.3 0.4 collective-permute-start.9
  54.7 0.0 copy-done.1
  54.7 0.0 copy-done.3
  54.7 4.1 %adam.3 = (f32[3,8,4,128,128]{4,3,2,1,0:T(8,128)}, f32[3,8,4,128,128]{4,3,2,1,0:T(8,128)}, f32[3,8,4,128,128]{4,3,2,1,0:T(8,128)}) custom-call(s32[3,4,8]{2,1,0:T(4,128)S(1)} %copy-done.1, s32[3,8]{1,0:T(4,128)S(1)} %copy-done.3, bf16[32,8192]{1,0:T(8,128)(2,1)S(1)} %get-tuple-element.73.left, bf16[32,1024]{1,0:T(8,128)(2,1)S(1)} %get-tuple-element.74.right, ...), custom_call_target="tpu_custom_call" | custom-call | bytes 6291456 | tf_op jit(solution)/shard_map/adam/pallas_call | solution.py:339
  58.8 1.1 %collective-permute-done.9 = bf16[8,8192]{1,0:T(8,128)(2,1)S(1)} collective-permute-done((bf16[8,8192]{1,0:T(8,128)(2,1)S(1)}, bf16[8,8192]{1,0:T(8,128)(2,1)S(1)}, u32[]{:S(2)}, u32[]{:S(2)}) %collective-permute-start.9) | collective-permute-done | bytes 131104 | tf_op jit(solution)/shard_map/ppermute | solution.py:353
  59.9 2.5 %collective-permute-start.10 = (bf16[4,8192]{1,0:T(4,128)(2,1)S(1)}, bf16[4,8192]{1,0:T(4,128)(2,1)S(1)}, u32[]{:S(2)}, u32[]{:S(2)}) collective-permute-start(bf16[4,8192]{1,0:T(4,128)(2,1)S(1)} %slice.38), channel_id=1, source_target_pairs={{0,8},{1,9},{2,10},{3,11},{4,12},{5,13},{6,14},{7,15},{8,0},{9,1},... | collective-permute-start | bytes 196616 | tf_op jit(solution)/shard_map/ppermute | solution.py:353
  62.4 4.1 %adam.4 = (f32[3,8,4,128,128]{4,3,2,1,0:T(8,128)}, f32[3,8,4,128,128]{4,3,2,1,0:T(8,128)}, f32[3,8,4,128,128]{4,3,2,1,0:T(8,128)}) custom-call(s32[3,4,8]{2,1,0:T(4,128)S(1)} %copy-done.1, s32[3,8]{1,0:T(4,128)S(1)} %copy-done.3, bf16[32,8192]{1,0:T(8,128)(2,1)S(1)} %get-tuple-element.73.left, ...), custom_call_target="tpu_custom_call", output_to_operand_aliasing={{0}: (7, {}), {1}: (8, {}), {2}: (9, {})} | custom-call | bytes 6291456 | tf_op jit(solution)/shard_map/adam/pallas_call | solution.py:339
  66.5 0.0 collective-permute-done.10
  66.6 2.0 %collective-permute-start.11 = (bf16[2,8192]{1,0:T(2,128)(2,1)S(1)}, bf16[2,8192]{1,0:T(2,128)(2,1)S(1)}, u32[]{:S(2)}, u32[]{:S(2)}) collective-permute-start(bf16[2,8192]{1,0:T(2,128)(2,1)S(1)} %slice.39), channel_id=1, source_target_pairs={{0,2},{1,3},{2,0},{3,1},{4,6},{5,7},{6,4},{7,5},{8,10},{9,11},{10,... | collective-permute-start | bytes 98312 | tf_op jit(solution)/shard_map/ppermute | solution.py:353
  68.7 4.1 %adam.5 = (f32[3,8,4,128,128]{4,3,2,1,0:T(8,128)}, f32[3,8,4,128,128]{4,3,2,1,0:T(8,128)}, f32[3,8,4,128,128]{4,3,2,1,0:T(8,128)}) custom-call(s32[3,4,8]{2,1,0:T(4,128)S(1)} %copy-done.1, s32[3,8]{1,0:T(4,128)S(1)} %copy-done.3, bf16[32,1024]{1,0:T(8,128)(2,1)S(1)} %get-tuple-element.86.left, ...), custom_call_target="tpu_custom_call", output_to_operand_aliasing={{0}: (7, {}), {1}: (8, {}), {2}: (9, {})} | custom-call | bytes 6291456 | tf_op jit(solution)/shard_map/adam/pallas_call | solution.py:339
  72.7 0.0 collective-permute-done.11
  72.7 0.7 convert_add_fusion.2
  (7 shorter events, 0.2 us)
Async XLA Ops:
  0.6 6.1 %collective-permute-start = (bf16[2,8192]{1,0:T(2,128)(2,1)}, bf16[2,8192]{1,0:T(2,128)(2,1)S(1)}, u32[]{:S(2)}, u32[]{:S(2)}) collective-permute-start(bf16[2,8192]{1,0:T(2,128)(2,1)} %refs_0_.1), channel_id=1, source_target_pairs={{0,2},{1,3},{2,0},{3,1},{4,6},{5,7},{6,4},{7,5},{8,10},{9,11},{10,... | collective-permute-start | bytes 98312 | tf_op jit(solution)/shard_map/ppermute | solution.py:353
  3.6 4.1 %collective-permute-start.1 = (bf16[2,8192]{1,0:T(2,128)(2,1)}, bf16[2,8192]{1,0:T(2,128)(2,1)S(1)}, u32[]{:S(2)}, u32[]{:S(2)}) collective-permute-start(bf16[2,8192]{1,0:T(2,128)(2,1)} %refs_1_.1), channel_id=1, source_target_pairs={{0,2},{1,3},{2,0},{3,1},{4,6},{5,7},{6,4},{7,5},{8,10},{9,11},{10,... | collective-permute-start | bytes 98312 | tf_op jit(solution)/shard_map/ppermute | solution.py:353
  6.7 11.3 %copy-start = (s32[3,4,8]{2,1,0:T(4,128)}, s32[3,4,8]{2,1,0:T(4,128)S(1)}, u32[]{:S(2)}) copy-start(s32[3,4,8]{2,1,0:T(4,128)S(1)} %get-tuple-element.85.kept) | copy-start | bytes 1156
  6.7 11.3 %copy-start.2 = (s32[3,8]{1,0:T(4,128)}, s32[3,8]{1,0:T(4,128)S(1)}, u32[]{:S(2)}) copy-start(s32[3,8]{1,0:T(4,128)S(1)} %get-tuple-element.49.counts) | copy-start | bytes 292
  7.8 7.4 %collective-permute-start.2 = (bf16[4,8192]{1,0:T(4,128)(2,1)S(1)}, bf16[4,8192]{1,0:T(4,128)(2,1)S(1)}, u32[]{:S(2)}, u32[]{:S(2)}) collective-permute-start(bf16[4,8192]{1,0:T(4,128)(2,1)S(1)} %pad_maximum_fusion.4), channel_id=1, source_target_pairs={{0,8},{1,9},{2,10},{3,11},{4,12},{5,13},{6,14},{7,15},{8,0},{9,1},... | collective-permute-start | bytes 196616 | tf_op jit(solution)/shard_map/ppermute | solution.py:353
  10.5 5.4 %collective-permute-start.3 = (bf16[4,8192]{1,0:T(4,128)(2,1)S(1)}, bf16[4,8192]{1,0:T(4,128)(2,1)S(1)}, u32[]{:S(2)}, u32[]{:S(2)}) collective-permute-start(bf16[4,8192]{1,0:T(4,128)(2,1)S(1)} %pad_maximum_fusion.5), channel_id=1, source_target_pairs={{0,8},{1,9},{2,10},{3,11},{4,12},{5,13},{6,14},{7,15},{8,0},{9,1},... | collective-permute-start | bytes 196616 | tf_op jit(solution)/shard_map/ppermute | solution.py:353
  15.9 6.6 %collective-permute-start.4 = (bf16[8,8192]{1,0:T(8,128)(2,1)S(1)}, bf16[8,8192]{1,0:T(8,128)(2,1)S(1)}, u32[]{:S(2)}, u32[]{:S(2)}) collective-permute-start(bf16[8,8192]{1,0:T(8,128)(2,1)S(1)} %pad_maximum_fusion.2), channel_id=1, source_target_pairs={{0,4},{1,5},{2,6},{3,7},{4,0},{5,1},{6,2},{7,3},{8,12},{9,13},{10,... | collective-permute-start | bytes 393224 | tf_op jit(solution)/shard_map/ppermute | solution.py:353
  17.4 6.4 %collective-permute-start.5 = (bf16[8,8192]{1,0:T(8,128)(2,1)S(1)}, bf16[8,8192]{1,0:T(8,128)(2,1)S(1)}, u32[]{:S(2)}, u32[]{:S(2)}) collective-permute-start(bf16[8,8192]{1,0:T(8,128)(2,1)S(1)} %pad_maximum_fusion.3), channel_id=1, source_target_pairs={{0,4},{1,5},{2,6},{3,7},{4,0},{5,1},{6,2},{7,3},{8,12},{9,13},{10,... | collective-permute-start | bytes 393224 | tf_op jit(solution)/shard_map/ppermute | solution.py:353
  23.8 30.9 %copy-start.1 = (s32[3,4,8]{2,1,0:T(4,128)S(1)}, s32[3,4,8]{2,1,0:T(4,128)}, u32[]{:S(2)}) copy-start(s32[3,4,8]{2,1,0:T(4,128)} %copy-done) | copy-start | bytes 1156
  23.8 30.9 %copy-start.3 = (s32[3,8]{1,0:T(4,128)S(1)}, s32[3,8]{1,0:T(4,128)}, u32[]{:S(2)}) copy-start(s32[3,8]{1,0:T(4,128)} %copy-done.2) | copy-start | bytes 292
  23.8 1.6 %collective-permute-start.6 = (bf16[16,8192]{1,0:T(8,128)(2,1)S(1)}, bf16[16,8192]{1,0:T(8,128)(2,1)S(1)}, u32[]{:S(2)}, u32[]{:S(2)}) collective-permute-start(bf16[16,8192]{1,0:T(8,128)(2,1)S(1)} %pad_maximum_fusion.tokens_0), channel_id=1, source_target_pairs={{0,1},{1,0},{2,3},{3,2},{4,5},{5,4},{6,7},{7,6},{8,9},{9,8},{10,11... | collective-permute-start | bytes 786440 | tf_op jit(solution)/shard_map/ppermute | solution.py:353
  23.9 1.9 %collective-permute-start.7 = (bf16[16,8192]{1,0:T(8,128)(2,1)S(1)}, bf16[16,8192]{1,0:T(8,128)(2,1)S(1)}, u32[]{:S(2)}, u32[]{:S(2)}) collective-permute-start(bf16[16,8192]{1,0:T(8,128)(2,1)S(1)} %pad_maximum_fusion.1.cotangent_0), channel_id=1, source_target_pairs={{0,1},{1,0},{2,3},{3,2},{4,5},{5,4},{6,7},{7,6},{8,9},{9,8},{10,11... | collective-permute-start | bytes 786440 | tf_op jit(solution)/shard_map/ppermute | solution.py:353
  52.6 1.6 %collective-permute-start.8 = (bf16[16,8192]{1,0:T(8,128)(2,1)S(1)}, bf16[16,8192]{1,0:T(8,128)(2,1)S(1)}, u32[]{:S(2)}, u32[]{:S(2)}) collective-permute-start(bf16[16,8192]{1,0:T(8,128)(2,1)S(1)} %get-tuple-element.64), channel_id=1, source_target_pairs={{0,1},{1,0},{2,3},{3,2},{4,5},{5,4},{6,7},{7,6},{8,9},{9,8},{10,11... | collective-permute-start | bytes 786440 | tf_op jit(solution)/shard_map/ppermute | solution.py:353
  54.3 5.6 %collective-permute-start.9 = (bf16[8,8192]{1,0:T(8,128)(2,1)S(1)}, bf16[8,8192]{1,0:T(8,128)(2,1)S(1)}, u32[]{:S(2)}, u32[]{:S(2)}) collective-permute-start(bf16[8,8192]{1,0:T(8,128)(2,1)S(1)} %slice.37), channel_id=1, source_target_pairs={{0,4},{1,5},{2,6},{3,7},{4,0},{5,1},{6,2},{7,3},{8,12},{9,13},{10,... | collective-permute-start | bytes 393224 | tf_op jit(solution)/shard_map/ppermute | solution.py:353
  59.9 6.6 %collective-permute-start.10 = (bf16[4,8192]{1,0:T(4,128)(2,1)S(1)}, bf16[4,8192]{1,0:T(4,128)(2,1)S(1)}, u32[]{:S(2)}, u32[]{:S(2)}) collective-permute-start(bf16[4,8192]{1,0:T(4,128)(2,1)S(1)} %slice.38), channel_id=1, source_target_pairs={{0,8},{1,9},{2,10},{3,11},{4,12},{5,13},{6,14},{7,15},{8,0},{9,1},... | collective-permute-start | bytes 196616 | tf_op jit(solution)/shard_map/ppermute | solution.py:353
  66.6 6.1 %collective-permute-start.11 = (bf16[2,8192]{1,0:T(2,128)(2,1)S(1)}, bf16[2,8192]{1,0:T(2,128)(2,1)S(1)}, u32[]{:S(2)}, u32[]{:S(2)}) collective-permute-start(bf16[2,8192]{1,0:T(2,128)(2,1)S(1)} %slice.39), channel_id=1, source_target_pairs={{0,2},{1,3},{2,0},{3,1},{4,6},{5,7},{6,4},{7,5},{8,10},{9,11},{10,... | collective-permute-start | bytes 98312 | tf_op jit(solution)/shard_map/ppermute | solution.py:353

commit v2 on v1

--- a/solution.py
+++ b/solution.py
@@ -21,6 +21,10 @@
 
 def in_vmem(*arrays):
     return [pltpu.with_memory_space_constraint(array, pltpu.VMEM) for array in arrays]
+
+
+def in_smem(*arrays):
+    return [pltpu.with_memory_space_constraint(array, pltpu.SMEM) for array in arrays]
 
 
 def dot_rows(left, right):
@@ -66,7 +70,11 @@
     kinds = [array.dtype for array in whole] + [blocks.dtype] * blocks.shape[0]
     return pl.pallas_call(
         functools.partial(enter_kernel, len(whole)),
-        out_shape=tuple(pltpu.VMEM(*out) for out in zip(shapes, kinds)),
+        out_shape=tuple(
+            (pltpu.SMEM if kind == jnp.int32 else pltpu.VMEM)(shape, kind)
+            for shape, kind in zip(shapes, kinds)
+        ),
+        out_specs=tuple(SMEM_SPEC if kind == jnp.int32 else VMEM_SPEC for kind in kinds),
         in_specs=[HBM_SPEC] * len(arrays),
         scratch_shapes=[pltpu.SemaphoreType.DMA((len(shapes),))],
         compiler_params=params(2 * MIB),
@@ -76,14 +84,19 @@
 
 def add_column_blocks(which, kept, counts, delta, ref, offset, first, size):
     tiles, slots, side = delta.shape[:3]
-    for t in range(tiles):
+
+    def tile(t, carry):
         for k in range(slots):
             row = kept[which, k, t] * side - offset
 
             @pl.when((k < counts[which, t]) & (row >= first) & (row < first + size))
             def _():
                 rows = pl.ds(pl.multiple_of(row, side), side)
-                add_block(ref, rows, slice(t * side, (t + 1) * side), delta[t, k])
+                add_block(ref, rows, chunk(t, side), delta[t, k])
+
+        return carry
+
+    lax.fori_loop(0, tiles, tile, 0)
 
 
 def patch_kernel(which, offset, step, kept, counts, delta, weight, out, sems):
@@ -102,7 +115,7 @@
 
 def patched(which, offset, height, kept, counts, delta, weight):
     units = weight.shape[1]
-    step = height // 2
+    step = height // 4
     return pl.pallas_call(
         functools.partial(patch_kernel, which, offset, step),
         out_shape=pltpu.VMEM((height, units), BF16),
@@ -111,7 +124,7 @@
         compiler_params=params(4 * MIB),
         cost_estimate=cost(0, 2 * height * units),
         name="patch",
-    )(kept, counts, *in_vmem(delta), *in_hbm(weight))
+    )(*in_smem(kept, counts), *in_vmem(delta), *in_hbm(weight))
 
 
 def moment_copies(which, sources, targets, sems, row=0):
@@ -248,8 +261,8 @@
 
     def input_part(gate_eff, offset, i, carry):
         cols = chunk(offset // step + i, step)
-        both = dot_rows(gate_grad[...], gate_eff[chunk(i, step), :])
-        both += dot_rows(up_grad[...], up_eff[cols, :])
+        both = dot_rows(gate_eff[chunk(i, step), :], gate_grad[...])
+        both = (both + dot_rows(up_eff[cols, :], up_grad[...])).T
         keep[:, cols] = both[:half]
         send[:, cols] = both[half:].astype(BF16)
         return carry
@@ -266,7 +279,7 @@
     shape = first.shape
     tiles, side = shape[1], shape[-1]
     height, span = min(2, tiles) * side, width // 2
-    wide, step = width // 4, width // 8
+    wide, step = width // 4, width // 4
     grad = pltpu.VMEM((rows, units), BF16)
     return pl.pallas_call(
         functools.partial(layer_kernel, wide, step),
@@ -294,8 +307,7 @@
         cost_estimate=cost(10 * rows * width * units, 10 * width * units),
         name="layer",
     )(
-        kept,
-        counts,
+        *in_smem(kept, counts),
         *in_vmem(*tokens, *cotangent, *gate_eff, *deltas[1:]),
         *in_hbm(up_weight, down_weight, first, second),
     )
@@ -346,7 +358,7 @@
         compiler_params=params(8 * MIB),
         cost_estimate=cost(0, 12 * delta.size),
         name="adam",
-    )(kept, counts, *in_vmem(left, right, delta, *moment_pair), *in_hbm(*done))
+    )(*in_smem(kept, counts), *in_vmem(left, right, delta, *moment_pair), *in_hbm(*done))
 
 
 def exchange(value, distance, size):
@@ -355,7 +367,7 @@
 
 def exchange_order(size):
     distances = [1 << bit for bit in range(size.bit_length() - 1)]
-    return distances[1:2] + distances[:1:-1] + distances[:1]
+    return distances[::-1]
 
 
 def after(value, *others):

time: 73.5 us -> 68.8 us (0.936)
  Pallas kernels: 50.9 us -> 46.3 us
    pallas_call x3, Pallas kernels: 12.2 us -> 10.2 us  [adam(): pl.pallas_call(functools.partial(adam_kernel, which), out_shape=(out, out...]
    pallas_call x1, Pallas kernels: 26.8 us -> 25.4 us  [layer(): pl.pallas_call(functools.partial(layer_kernel, wide, step), out_shape=(pl...]
    pallas_call x2, Pallas kernels: 8.94 us -> 7.63 us  [patched(): pl.pallas_call(functools.partial(patch_kernel, which, offset, step), out_...]
  transfers between devices with their start and end apart: 12 -> 12, of which waited for: 7 -> 6; matrix products, arithmetic and copies ran while one was open for 0% -> 0% of each run, Pallas kernels for 33% -> 30%
where the time goes in v2:
time: 68.8 us; the launch traced here: 68.7 us
  Pallas kernels  46.3 us (67%)
  starting transfers between devices  14.4 us (21%)
  waiting for transfers between devices  6.06 us (9%)
  other arithmetic  1.09 us (2%)
  between operations  0.82 us (1%)
    pallas_call x1, Pallas kernels, layer(): pl.pallas_call(functools.partial(layer_kernel, wide, step), out_shape=(pl...  25.4 us
    ppermute x12, starting transfers between devices, exchange(): return lax.ppermute(value, 'dp', [(i, i ^ distance) for i in range(size)])  14.4 us
    pallas_call x3, Pallas kernels, adam(): pl.pallas_call(functools.partial(adam_kernel, which), out_shape=(out, out...  10.2 us
    pallas_call x2, Pallas kernels, patched(): pl.pallas_call(functools.partial(patch_kernel, which, offset, step), out_...  7.63 us
    ppermute x12, waiting for transfers between devices, exchange(): return lax.ppermute(value, 'dp', [(i, i ^ distance) for i in range(size)])  6.06 us
    pallas_call x1, Pallas kernels, into_vmem(): pl.pallas_call(functools.partial(enter_kernel, len(whole)), out_shape=tup...  2.95 us
  transfers between devices with their start and end apart: 12, of which 6 were waited for; matrix products, arithmetic and copies ran while one was open for 0% of the time, Pallas kernels for 30%

profile of v2, /device:TPU:0, one launch (start us, length us, event | category | flops | bytes accessed | tf_op | source)
XLA Modules:
  0.0 68.7 jit_solution(6844957518435672700)
XLA Ops:
  0.6 4.1 %collective-permute-start = (bf16[2,8192]{1,0:T(2,128)(2,1)}, bf16[2,8192]{1,0:T(2,128)(2,1)S(1)}, u32[]{:S(2)}, u32[]{:S(2)}) collective-permute-start(bf16[2,8192]{1,0:T(2,128)(2,1)} %refs_0_.1), channel_id=1, source_target_pairs={{0,8},{1,9},{2,10},{3,11},{4,12},{5,13},{6,14},{7,15},{8,0},{9,1},... | collective-permute-start | bytes 98312 | tf_op jit(solution)/shard_map/ppermute | solution.py:365
  4.7 0.1 collective-permute-start.1
  4.8 3.0 %enter.1 = (bf16[2,8192]{1,0:T(2,128)(2,1)S(1)}, bf16[2,8192]{1,0:T(2,128)(2,1)S(1)}, s32[3,4,8]{2,1,0:T(4,128)S(4)}, s32[3,8]{1,0:T(4,128)S(4)}, f32[8,4,128,12...) custom-call(bf16[2,8192]{1,0:T(2,128)(2,1)} %refs_0_.1, bf16[2,8192]{1,0:T(2,128)(2,1)} %refs_1_.1, ...), custom_call_target="tpu_custom_call" | custom-call | tf_op jit(solution)/shard_map/enter/pallas_call | solution.py:71
  7.8 0.0 collective-permute-done
  7.8 0.1 pad_maximum_fusion.4
  7.9 1.9 %collective-permute-done.1 = bf16[2,8192]{1,0:T(2,128)(2,1)S(1)} collective-permute-done((bf16[2,8192]{1,0:T(2,128)(2,1)}, bf16[2,8192]{1,0:T(2,128)(2,1)S(1)}, u32[]{:S(2)}, u32[]{:S(2)}) %collective-permute-start.1) | collective-permute-done | bytes 32800 | tf_op jit(solution)/shard_map/ppermute | solution.py:365
  9.8 0.1 pad_maximum_fusion.5
  9.8 1.6 %collective-permute-start.2 = (bf16[4,8192]{1,0:T(4,128)(2,1)S(1)}, bf16[4,8192]{1,0:T(4,128)(2,1)S(1)}, u32[]{:S(2)}, u32[]{:S(2)}) collective-permute-start(bf16[4,8192]{1,0:T(4,128)(2,1)S(1)} %pad_maximum_fusion.4), channel_id=1, source_target_pairs={{0,4},{1,5},{2,6},{3,7},{4,0},{5,1},{6,2},{7,3},{8,12},{9,13},{10,... | collective-permute-start | bytes 196616 | tf_op jit(solution)/shard_map/ppermute | solution.py:365
  11.5 0.4 collective-permute-start.3
  11.9 3.9 %patch.2.gate_0 = bf16[4096,1024]{1,0:T(8,128)(2,1)S(1)} custom-call(s32[3,4,8]{2,1,0:T(4,128)S(4)} %get-tuple-element.85.kept, s32[3,8]{1,0:T(4,128)S(4)} %get-tuple-element.49.counts, f32[8,4,128,128]{3,2,1,0:T(8,128)S(1)} %get-tuple-element.52.delta, bf16[8192,1024]{1,0:T(8,128)(2,1)} %weight.3), custom_call_target="tpu_custom_call" | custom-call | bytes 8388608 | tf_op jit(solution)/shard_map/patch/pallas_call | solution.py:119
  15.8 0.0 collective-permute-done.2
  15.9 0.1 pad_maximum_fusion.2
  15.9 0.0 collective-permute-done.3
  15.9 0.1 pad_maximum_fusion.3
  16.0 1.5 %collective-permute-start.4 = (bf16[8,8192]{1,0:T(8,128)(2,1)S(1)}, bf16[8,8192]{1,0:T(8,128)(2,1)S(1)}, u32[]{:S(2)}, u32[]{:S(2)}) collective-permute-start(bf16[8,8192]{1,0:T(8,128)(2,1)S(1)} %pad_maximum_fusion.2), channel_id=1, source_target_pairs={{0,2},{1,3},{2,0},{3,1},{4,6},{5,7},{6,4},{7,5},{8,10},{9,11},{10,... | collective-permute-start | bytes 393224 | tf_op jit(solution)/shard_map/ppermute | solution.py:365
  17.5 0.6 collective-permute-start.5
  18.1 3.7 %patch.3.gate_1 = bf16[4096,1024]{1,0:T(8,128)(2,1)S(1)} custom-call(s32[3,4,8]{2,1,0:T(4,128)S(4)} %get-tuple-element.85.kept, s32[3,8]{1,0:T(4,128)S(4)} %get-tuple-element.49.counts, f32[8,4,128,128]{3,2,1,0:T(8,128)S(1)} %get-tuple-element.52.delta, bf16[8192,1024]{1,0:T(8,128)(2,1)} %weight.3), custom_call_target="tpu_custom_call" | custom-call | bytes 8388608 | tf_op jit(solution)/shard_map/patch/pallas_call | solution.py:119
  21.8 0.0 collective-permute-done.4
  21.9 0.6 collective-permute-done.5
  22.5 0.1 collective-permute-start.6
  22.6 0.5 collective-permute-start.7
  23.1 1.0 %collective-permute-done.6.tokens_1 = bf16[16,8192]{1,0:T(8,128)(2,1)S(1)} collective-permute-done((bf16[16,8192]{1,0:T(8,128)(2,1)S(1)}, bf16[16,8192]{1,0:T(8,128)(2,1)S(1)}, u32[]{:S(2)}, u32[]{:S(2)}) %collective-permute-start.6) | collective-permute-done | bytes 262176 | tf_op jit(solution)/shard_map/ppermute | solution.py:365
  24.1 0.4 collective-permute-done.7.cotangent_1
  24.5 25.4 %layer.1 = (f32[16,8192]{1,0:T(8,128)S(1)}, bf16[16,8192]{1,0:T(8,128)(2,1)S(1)}, bf16[32,8192]{1,0:T(8,128)(2,1)S(1)}, bf16[32,8192]{1,0:T(8,128)(2,1)S(1)}, bf...) custom-call(s32[3,4,8]{2,1,0:T(4,128)S(4)} %get-tuple-element.85.kep, ...), custom_call_target="tpu_custom_call" | custom-call | flops 2684354560 | bytes 83886080 | tf_op jit(solution)/shard_map/layer/pallas_call | solution.py:284
  49.9 0.2 collective-permute-start.8
  50.1 1.4 %collective-permute-done.8 = bf16[16,8192]{1,0:T(8,128)(2,1)S(1)} collective-permute-done((bf16[16,8192]{1,0:T(8,128)(2,1)S(1)}, bf16[16,8192]{1,0:T(8,128)(2,1)S(1)}, u32[]{:S(2)}, u32[]{:S(2)}) %collective-permute-start.8) | collective-permute-done | bytes 262176 | tf_op jit(solution)/shard_map/ppermute | solution.py:365
  51.6 1.5 %collective-permute-start.9 = (bf16[8,8192]{1,0:T(8,128)(2,1)S(1)}, bf16[8,8192]{1,0:T(8,128)(2,1)S(1)}, u32[]{:S(2)}, u32[]{:S(2)}) collective-permute-start(bf16[8,8192]{1,0:T(8,128)(2,1)S(1)} %slice.37), channel_id=1, source_target_pairs={{0,2},{1,3},{2,0},{3,1},{4,6},{5,7},{6,4},{7,5},{8,10},{9,11},{10,... | collective-permute-start | bytes 393224 | tf_op jit(solution)/shard_map/ppermute | solution.py:365
  53.0 3.4 %adam.3 = (f32[3,8,4,128,128]{4,3,2,1,0:T(8,128)}, f32[3,8,4,128,128]{4,3,2,1,0:T(8,128)}, f32[3,8,4,128,128]{4,3,2,1,0:T(8,128)}) custom-call(s32[3,4,8]{2,1,0:T(4,128)S(4)} %get-tuple-element.85.kept, s32[3,8]{1,0:T(4,128)S(4)} %get-tuple-element.49.counts, bf16[32,8192]{1,0:T(8,128)(2,1)S(1)} %get-tuple-element.73.left, ...), custom_call_target="tpu_custom_call" | custom-call | bytes 6291456 | tf_op jit(solution)/shard_map/adam/pallas_call | solution.py:351
  56.5 0.7 %collective-permute-done.9 = bf16[8,8192]{1,0:T(8,128)(2,1)S(1)} collective-permute-done((bf16[8,8192]{1,0:T(8,128)(2,1)S(1)}, bf16[8,8192]{1,0:T(8,128)(2,1)S(1)}, u32[]{:S(2)}, u32[]{:S(2)}) %collective-permute-start.9) | collective-permute-done | bytes 131104 | tf_op jit(solution)/shard_map/ppermute | solution.py:365
  57.2 1.7 %collective-permute-start.10 = (bf16[4,8192]{1,0:T(4,128)(2,1)S(1)}, bf16[4,8192]{1,0:T(4,128)(2,1)S(1)}, u32[]{:S(2)}, u32[]{:S(2)}) collective-permute-start(bf16[4,8192]{1,0:T(4,128)(2,1)S(1)} %slice.38), channel_id=1, source_target_pairs={{0,4},{1,5},{2,6},{3,7},{4,0},{5,1},{6,2},{7,3},{8,12},{9,13},{10,... | collective-permute-start | bytes 196616 | tf_op jit(solution)/shard_map/ppermute | solution.py:365
  59.0 3.4 %adam.4 = (f32[3,8,4,128,128]{4,3,2,1,0:T(8,128)}, f32[3,8,4,128,128]{4,3,2,1,0:T(8,128)}, f32[3,8,4,128,128]{4,3,2,1,0:T(8,128)}) custom-call(s32[3,4,8]{2,1,0:T(4,128)S(4)} %get-tuple-element.85.kept, s32[3,8]{1,0:T(4,128)S(4)} %get-tuple-element.49.counts, ...), custom_call_target="tpu_custom_call", output_to_operand_aliasing={{0}: (7, {}), {1}: (8, {}), {2}: (9, {})} | custom-call | bytes 6291456 | tf_op jit(solution)/shard_map/adam/pallas_call | solution.py:351
  62.4 0.0 collective-permute-done.10
  62.5 2.1 %collective-permute-start.11 = (bf16[2,8192]{1,0:T(2,128)(2,1)S(1)}, bf16[2,8192]{1,0:T(2,128)(2,1)S(1)}, u32[]{:S(2)}, u32[]{:S(2)}) collective-permute-start(bf16[2,8192]{1,0:T(2,128)(2,1)S(1)} %slice.39), channel_id=1, source_target_pairs={{0,8},{1,9},{2,10},{3,11},{4,12},{5,13},{6,14},{7,15},{8,0},{9,1},... | collective-permute-start | bytes 98312 | tf_op jit(solution)/shard_map/ppermute | solution.py:365
  64.6 3.4 %adam.5 = (f32[3,8,4,128,128]{4,3,2,1,0:T(8,128)}, f32[3,8,4,128,128]{4,3,2,1,0:T(8,128)}, f32[3,8,4,128,128]{4,3,2,1,0:T(8,128)}) custom-call(s32[3,4,8]{2,1,0:T(4,128)S(4)} %get-tuple-element.85.kept, s32[3,8]{1,0:T(4,128)S(4)} %get-tuple-element.49.counts, ...), custom_call_target="tpu_custom_call", output_to_operand_aliasing={{0}: (7, {}), {1}: (8, {}), {2}: (9, {})} | custom-call | bytes 6291456 | tf_op jit(solution)/shard_map/adam/pallas_call | solution.py:351
  68.0 0.0 collective-permute-done.11
  68.0 0.7 convert_add_fusion.2
  (8 shorter events, 0.2 us)
Async XLA Ops:
  0.6 7.1 %collective-permute-start = (bf16[2,8192]{1,0:T(2,128)(2,1)}, bf16[2,8192]{1,0:T(2,128)(2,1)S(1)}, u32[]{:S(2)}, u32[]{:S(2)}) collective-permute-start(bf16[2,8192]{1,0:T(2,128)(2,1)} %refs_0_.1), channel_id=1, source_target_pairs={{0,8},{1,9},{2,10},{3,11},{4,12},{5,13},{6,14},{7,15},{8,0},{9,1},... | collective-permute-start | bytes 98312 | tf_op jit(solution)/shard_map/ppermute | solution.py:365
  4.7 5.0 %collective-permute-start.1 = (bf16[2,8192]{1,0:T(2,128)(2,1)}, bf16[2,8192]{1,0:T(2,128)(2,1)S(1)}, u32[]{:S(2)}, u32[]{:S(2)}) collective-permute-start(bf16[2,8192]{1,0:T(2,128)(2,1)} %refs_1_.1), channel_id=1, source_target_pairs={{0,8},{1,9},{2,10},{3,11},{4,12},{5,13},{6,14},{7,15},{8,0},{9,1},... | collective-permute-start | bytes 98312 | tf_op jit(solution)/shard_map/ppermute | solution.py:365
  9.8 6.0 %collective-permute-start.2 = (bf16[4,8192]{1,0:T(4,128)(2,1)S(1)}, bf16[4,8192]{1,0:T(4,128)(2,1)S(1)}, u32[]{:S(2)}, u32[]{:S(2)}) collective-permute-start(bf16[4,8192]{1,0:T(4,128)(2,1)S(1)} %pad_maximum_fusion.4), channel_id=1, source_target_pairs={{0,4},{1,5},{2,6},{3,7},{4,0},{5,1},{6,2},{7,3},{8,12},{9,13},{10,... | collective-permute-start | bytes 196616 | tf_op jit(solution)/shard_map/ppermute | solution.py:365
  11.5 4.5 %collective-permute-start.3 = (bf16[4,8192]{1,0:T(4,128)(2,1)S(1)}, bf16[4,8192]{1,0:T(4,128)(2,1)S(1)}, u32[]{:S(2)}, u32[]{:S(2)}) collective-permute-start(bf16[4,8192]{1,0:T(4,128)(2,1)S(1)} %pad_maximum_fusion.5), channel_id=1, source_target_pairs={{0,4},{1,5},{2,6},{3,7},{4,0},{5,1},{6,2},{7,3},{8,12},{9,13},{10,... | collective-permute-start | bytes 196616 | tf_op jit(solution)/shard_map/ppermute | solution.py:365
  16.0 5.8 %collective-permute-start.4 = (bf16[8,8192]{1,0:T(8,128)(2,1)S(1)}, bf16[8,8192]{1,0:T(8,128)(2,1)S(1)}, u32[]{:S(2)}, u32[]{:S(2)}) collective-permute-start(bf16[8,8192]{1,0:T(8,128)(2,1)S(1)} %pad_maximum_fusion.2), channel_id=1, source_target_pairs={{0,2},{1,3},{2,0},{3,1},{4,6},{5,7},{6,4},{7,5},{8,10},{9,11},{10,... | collective-permute-start | bytes 393224 | tf_op jit(solution)/shard_map/ppermute | solution.py:365
  17.5 5.0 %collective-permute-start.5 = (bf16[8,8192]{1,0:T(8,128)(2,1)S(1)}, bf16[8,8192]{1,0:T(8,128)(2,1)S(1)}, u32[]{:S(2)}, u32[]{:S(2)}) collective-permute-start(bf16[8,8192]{1,0:T(8,128)(2,1)S(1)} %pad_maximum_fusion.3), channel_id=1, source_target_pairs={{0,2},{1,3},{2,0},{3,1},{4,6},{5,7},{6,4},{7,5},{8,10},{9,11},{10,... | collective-permute-start | bytes 393224 | tf_op jit(solution)/shard_map/ppermute | solution.py:365
  22.5 1.6 %collective-permute-start.6 = (bf16[16,8192]{1,0:T(8,128)(2,1)S(1)}, bf16[16,8192]{1,0:T(8,128)(2,1)S(1)}, u32[]{:S(2)}, u32[]{:S(2)}) collective-permute-start(bf16[16,8192]{1,0:T(8,128)(2,1)S(1)} %pad_maximum_fusion.tokens_0), channel_id=1, source_target_pairs={{0,1},{1,0},{2,3},{3,2},{4,5},{5,4},{6,7},{7,6},{8,9},{9,8},{10,11... | collective-permute-start | bytes 786440 | tf_op jit(solution)/shard_map/ppermute | solution.py:365
  22.6 1.9 %collective-permute-start.7 = (bf16[16,8192]{1,0:T(8,128)(2,1)S(1)}, bf16[16,8192]{1,0:T(8,128)(2,1)S(1)}, u32[]{:S(2)}, u32[]{:S(2)}) collective-permute-start(bf16[16,8192]{1,0:T(8,128)(2,1)S(1)} %pad_maximum_fusion.1.cotangent_0), channel_id=1, source_target_pairs={{0,1},{1,0},{2,3},{3,2},{4,5},{5,4},{6,7},{7,6},{8,9},{9,8},{10,11... | collective-permute-start | bytes 786440 | tf_op jit(solution)/shard_map/ppermute | solution.py:365
  49.9 1.6 %collective-permute-start.8 = (bf16[16,8192]{1,0:T(8,128)(2,1)S(1)}, bf16[16,8192]{1,0:T(8,128)(2,1)S(1)}, u32[]{:S(2)}, u32[]{:S(2)}) collective-permute-start(bf16[16,8192]{1,0:T(8,128)(2,1)S(1)} %get-tuple-element.64), channel_id=1, source_target_pairs={{0,1},{1,0},{2,3},{3,2},{4,5},{5,4},{6,7},{7,6},{8,9},{9,8},{10,11... | collective-permute-start | bytes 786440 | tf_op jit(solution)/shard_map/ppermute | solution.py:365
  51.6 5.6 %collective-permute-start.9 = (bf16[8,8192]{1,0:T(8,128)(2,1)S(1)}, bf16[8,8192]{1,0:T(8,128)(2,1)S(1)}, u32[]{:S(2)}, u32[]{:S(2)}) collective-permute-start(bf16[8,8192]{1,0:T(8,128)(2,1)S(1)} %slice.37), channel_id=1, source_target_pairs={{0,2},{1,3},{2,0},{3,1},{4,6},{5,7},{6,4},{7,5},{8,10},{9,11},{10,... | collective-permute-start | bytes 393224 | tf_op jit(solution)/shard_map/ppermute | solution.py:365
  57.2 5.2 %collective-permute-start.10 = (bf16[4,8192]{1,0:T(4,128)(2,1)S(1)}, bf16[4,8192]{1,0:T(4,128)(2,1)S(1)}, u32[]{:S(2)}, u32[]{:S(2)}) collective-permute-start(bf16[4,8192]{1,0:T(4,128)(2,1)S(1)} %slice.38), channel_id=1, source_target_pairs={{0,4},{1,5},{2,6},{3,7},{4,0},{5,1},{6,2},{7,3},{8,12},{9,13},{10,... | collective-permute-start | bytes 196616 | tf_op jit(solution)/shard_map/ppermute | solution.py:365
  62.5 5.5 %collective-permute-start.11 = (bf16[2,8192]{1,0:T(2,128)(2,1)S(1)}, bf16[2,8192]{1,0:T(2,128)(2,1)S(1)}, u32[]{:S(2)}, u32[]{:S(2)}) collective-permute-start(bf16[2,8192]{1,0:T(2,128)(2,1)S(1)} %slice.39), channel_id=1, source_target_pairs={{0,8},{1,9},{2,10},{3,11},{4,12},{5,13},{6,14},{7,15},{8,0},{9,1},... | collective-permute-start | bytes 98312 | tf_op jit(solution)/shard_map/ppermute | solution.py:365

commit v3 on v2

--- a/solution.py
+++ b/solution.py
@@ -51,8 +51,47 @@
     ref[rows, cols] = (ref[rows, cols].astype(F32) + block).astype(BF16)
 
 
-def enter_kernel(count, *refs):
-    blocks, targets, sems = refs[count], refs[count + 1 : -1], refs[-1]
+PARTS = 8
+
+
+def list_live(per_part, kept, counts, begins, entries):
+    _, slots, tiles = kept.shape
+    for m in range(entries.shape[0]):
+
+        def each(step, m=m):
+            def tile(t, carry):
+                for k in range(slots):
+
+                    @pl.when(k < counts[m, t])
+                    def _():
+                        step(lax.div(kept[m, k, t], per_part), t * slots + k)
+
+                return carry
+
+            lax.fori_loop(0, tiles, tile, 0)
+
+        def count(part, entry, m=m):
+            begins[m, part + 1] += 1
+
+        def place(part, entry, m=m):
+            at = begins[m, part]
+            entries[m, at] = entry
+            begins[m, part] = at + 1
+
+        for part in range(PARTS + 1):
+            begins[m, part] = 0
+        each(count)
+        for part in range(PARTS):
+            begins[m, part + 1] += begins[m, part]
+        each(place)
+        for part in range(PARTS, 0, -1):
+            begins[m, part] = begins[m, part - 1]
+        begins[m, 0] = 0
+
+
+def enter_kernel(per_part, count, *refs):
+    blocks, targets, sems = refs[count], refs[count + 1 : -3], refs[-1]
+    begins, entries = refs[-3:-1]
     sources = [*refs[:count], *(blocks.at[i] for i in range(blocks.shape[0]))]
     copies = [
         pltpu.make_async_copy(source, target, sems.at[i])
@@ -60,46 +99,49 @@
     ]
     for copy in copies:
         copy.start()
-    for copy in copies:
+    for copy in copies[:count]:
+        copy.wait()
+    list_live(per_part, targets[count - 2], targets[count - 1], begins, entries)
+    for copy in copies[count:]:
         copy.wait()
 
 
 def into_vmem(*arrays):
     *whole, blocks = arrays
+    _, tiles, slots, side, _ = blocks.shape
     shapes = [array.shape for array in whole] + [blocks.shape[1:]] * blocks.shape[0]
     kinds = [array.dtype for array in whole] + [blocks.dtype] * blocks.shape[0]
+    shapes += [(2, PARTS + 1), (2, tiles * slots)]
+    kinds += [jnp.int32] * 2
+    per_part = whole[0].shape[1] // (PARTS * side)
     return pl.pallas_call(
-        functools.partial(enter_kernel, len(whole)),
+        functools.partial(enter_kernel, per_part, len(whole)),
         out_shape=tuple(
             (pltpu.SMEM if kind == jnp.int32 else pltpu.VMEM)(shape, kind)
             for shape, kind in zip(shapes, kinds)
         ),
         out_specs=tuple(SMEM_SPEC if kind == jnp.int32 else VMEM_SPEC for kind in kinds),
         in_specs=[HBM_SPEC] * len(arrays),
-        scratch_shapes=[pltpu.SemaphoreType.DMA((len(shapes),))],
+        scratch_shapes=[pltpu.SemaphoreType.DMA((len(shapes) - 2,))],
         compiler_params=params(2 * MIB),
         name="enter",
     )(*in_hbm(*arrays))
 
 
-def add_column_blocks(which, kept, counts, delta, ref, offset, first, size):
-    tiles, slots, side = delta.shape[:3]
-
-    def tile(t, carry):
-        for k in range(slots):
-            row = kept[which, k, t] * side - offset
-
-            @pl.when((k < counts[which, t]) & (row >= first) & (row < first + size))
-            def _():
-                rows = pl.ds(pl.multiple_of(row, side), side)
-                add_block(ref, rows, chunk(t, side), delta[t, k])
-
+def add_column_blocks(which, kept, begins, entries, delta, ref, offset, part, span):
+    slots, side = delta.shape[1:3]
+
+    def add(i, carry):
+        entry = entries[which, i]
+        t, k = lax.div(entry, slots), lax.rem(entry, slots)
+        row = kept[which, k, t] * side - offset
+        add_block(ref, pl.ds(pl.multiple_of(row, side), side), chunk(t, side), delta[t, k])
         return carry
 
-    lax.fori_loop(0, tiles, tile, 0)
-
-
-def patch_kernel(which, offset, step, kept, counts, delta, weight, out, sems):
+    lax.fori_loop(begins[which, part], begins[which, part + span], add, 0)
+
+
+def patch_kernel(which, offset, step, kept, begins, entries, delta, weight, out, sems):
     parts = out.shape[0] // step
 
     def part_copy(p):
@@ -110,21 +152,21 @@
         part_copy(p).start()
     for p in range(parts):
         part_copy(p).wait()
-        add_column_blocks(which, kept, counts, delta, out, offset, p * step, step)
-
-
-def patched(which, offset, height, kept, counts, delta, weight):
+        add_column_blocks(which, kept, begins, entries, delta, out, offset, offset // step + p, 1)
+
+
+def patched(which, offset, height, kept, lists, delta, weight):
     units = weight.shape[1]
-    step = height // 4
+    step = weight.shape[0] // PARTS
     return pl.pallas_call(
         functools.partial(patch_kernel, which, offset, step),
         out_shape=pltpu.VMEM((height, units), BF16),
-        in_specs=[SMEM_SPEC, SMEM_SPEC, VMEM_SPEC, HBM_SPEC],
+        in_specs=[SMEM_SPEC] * 3 + [VMEM_SPEC, HBM_SPEC],
         scratch_shapes=[pltpu.SemaphoreType.DMA((height // step,))],
         compiler_params=params(4 * MIB),
         cost_estimate=cost(0, 2 * height * units),
         name="patch",
-    )(*in_smem(kept, counts), *in_vmem(delta), *in_hbm(weight))
+    )(*in_smem(kept, *lists), *in_vmem(delta), *in_hbm(weight))
 
 
 def moment_copies(which, sources, targets, sems, row=0):
@@ -156,7 +198,7 @@
 
 
 def layer_kernel(
-    wide, step, kept, counts, tokens_0, tokens_1, cotangent_0, cotangent_1,
+    wide, step, kept, counts, begins, entries, tokens_0, tokens_1, cotangent_0, cotangent_1,
     gate_0, gate_1, up_delta, down_delta, up_weight, down_weight, first, second,
     keep, send, tokens, cotangent, hidden, gate_grad, up_grad, *refs,
 ):
@@ -212,7 +254,8 @@
     def forward_up(p, carry):
         part_copy(p).wait()
         start(p + flight)
-        add_column_blocks(1, kept, counts, up_delta, up_eff, 0, p * wide, wide)
+        span = wide * PARTS // width
+        add_column_blocks(1, kept, begins, entries, up_delta, up_eff, 0, p * span, span)
         product(up, up_eff, 0, p)
         return carry
 
@@ -273,7 +316,7 @@
         copy.wait()
 
 
-def layer(ahead, kept, counts, tokens, cotangent, gate_eff, deltas, up_weight, down_weight, first, second):
+def layer(ahead, kept, counts, lists, tokens, cotangent, gate_eff, deltas, up_weight, down_weight, first, second):
     rows, width = 2 * tokens[0].shape[0], tokens[0].shape[1]
     units = gate_eff[0].shape[1]
     shape = first.shape
@@ -293,7 +336,7 @@
             grad,
             *(pltpu.VMEM(shape[1:], F32),) * (2 * ahead),
         ),
-        in_specs=[SMEM_SPEC] * 2 + [VMEM_SPEC] * 8 + [HBM_SPEC] * 4,
+        in_specs=[SMEM_SPEC] * 4 + [VMEM_SPEC] * 8 + [HBM_SPEC] * 4,
         scratch_shapes=[
             pltpu.VMEM((width, units), BF16),
             pltpu.VMEM((3, height, span), BF16),
@@ -307,7 +350,7 @@
         cost_estimate=cost(10 * rows * width * units, 10 * width * units),
         name="layer",
     )(
-        *in_smem(kept, counts),
+        *in_smem(kept, counts, *lists),
         *in_vmem(*tokens, *cotangent, *gate_eff, *deltas[1:]),
         *in_hbm(up_weight, down_weight, first, second),
     )
@@ -367,7 +410,14 @@
 
 def exchange_order(size):
     distances = [1 << bit for bit in range(size.bit_length() - 1)]
-    return distances[::-1]
+    return distances[::-1], distances[1:2] + distances[:1:-1] + distances[:1]
+
+
+def joined(own, got, early):
+    if not early:
+        return jnp.concatenate([own, got], 0)
+    half = own.shape[0] // 2
+    return jnp.concatenate([own[:half], got[:half], own[half:], got[half:]], 0)
 
 
 def after(value, *others):
@@ -387,26 +437,28 @@
     first_moment,
     second_moment,
 ):
-    order = exchange_order(size)
+    order, other_order = exchange_order(size)
     raw = (tokens, cotangent)
-    tokens, cotangent, kept, counts, *deltas = into_vmem(
+    tokens, cotangent, kept, counts, *deltas, begins, entries = into_vmem(
         tokens, cotangent, kept_blocks.transpose(0, 2, 1), kept_counts, sparse_delta
     )
     half = gate_weight.shape[0] // 2
+    lists = (begins, entries)
     pair = (tokens, cotangent)
     gate_eff = []
-    for i, distance in enumerate(order):
-        got = tuple(exchange(rows, distance, size) for rows in (pair if i else raw))
+    for i, distances in enumerate(zip(order, other_order)):
+        sent = pair if i else raw
+        got = tuple(exchange(rows, distance, size) for rows, distance in zip(sent, distances))
         if max(len(order) - 3, 0) <= i < len(order) - 1:
             offset = len(gate_eff) * half
-            gate_eff.append(patched(0, offset, half, after(kept, *pair), counts, deltas[0], gate_weight))
+            gate_eff.append(patched(0, offset, half, after(kept, *pair), lists, deltas[0], gate_weight))
         if i < len(order) - 1:
-            pair = tuple(jnp.concatenate(both, 0) for both in zip(pair, got))
-            pair = after(pair, *deltas, *gate_eff[-1:])
+            pair = (joined(pair[0], got[0], False), joined(pair[1], got[1], i > 0))
+            pair = after(pair, *deltas, *lists, *gate_eff[-1:])
     tokens, cotangent = zip(pair, got)
     ahead = 3
     total, away, tokens, cotangent, hidden, gate_grad, up_grad, *fetched = layer(
-        ahead, kept, counts, tokens, cotangent, gate_eff, deltas, up_weight, down_weight, first_moment, second_moment
+        ahead, kept, counts, lists, tokens, cotangent, gate_eff, deltas, up_weight, down_weight, first_moment, second_moment
     )
     operands = ((tokens, gate_grad), (tokens, up_grad), (hidden, cotangent))
     news = ()

time: 68.8 us -> 66.3 us (0.964)
  waiting for transfers between devices: 6.06 us -> 3.61 us
  Pallas kernels: 46.3 us -> 44 us
  starting transfers between devices: 14.4 us -> 16.1 us
    ppermute x12, waiting for transfers between devices: 6.06 us -> 3.61 us  [exchange(): return lax.ppermute(value, 'dp', [(i, i ^ distance) for i in range(size)])]
    ppermute x12, starting transfers between devices: 14.4 us -> 16.1 us  [exchange(): return lax.ppermute(value, 'dp', [(i, i ^ distance) for i in range(size)])]
    pallas_call x1, Pallas kernels: 25.4 us -> 23.8 us  [layer(): pl.pallas_call(functools.partial(layer_kernel, wide, step), out_shape=(pl...]
  transfers between devices with their start and end apart: 12 -> 12, of which waited for: 6 -> 4; matrix products, arithmetic and copies ran while one was open for 0% -> 1% of each run, Pallas kernels for 30% -> 31%
where the time goes in v3:
time: 66.3 us; the launch traced here: 66.1 us
  Pallas kernels  44 us (66%)
  starting transfers between devices  16.1 us (24%)
  waiting for transfers between devices  3.61 us (5%)
  other arithmetic  1.32 us (2%)
  between operations  0.86 us (1%)
    pallas_call x1, Pallas kernels, layer(): pl.pallas_call(functools.partial(layer_kernel, wide, step), out_shape=(pl...  23.8 us
    ppermute x12, starting transfers between devices, exchange(): return lax.ppermute(value, 'dp', [(i, i ^ distance) for i in range(size)])  16.1 us
    pallas_call x3, Pallas kernels, adam(): pl.pallas_call(functools.partial(adam_kernel, which), out_shape=(out, out...  10.2 us
    pallas_call x2, Pallas kernels, patched(): pl.pallas_call(functools.partial(patch_kernel, which, offset, step), out_...  7.01 us
    ppermute x12, waiting for transfers between devices, exchange(): return lax.ppermute(value, 'dp', [(i, i ^ distance) for i in range(size)])  3.61 us
    pallas_call x1, Pallas kernels, into_vmem(): pl.pallas_call(functools.partial(enter_kernel, per_part, len(whole)), out...  2.95 us
  transfers between devices with their start and end apart: 12, of which 4 were waited for; matrix products, arithmetic and copies ran while one was open for 1% of the time, Pallas kernels for 31%

profile of v3, /device:TPU:0, one launch (start us, length us, event | category | flops | bytes accessed | tf_op | source)
XLA Modules:
  0.0 66.1 jit_solution(1401470680526541565)
XLA Ops:
  0.6 4.1 %collective-permute-start = (bf16[2,8192]{1,0:T(2,128)(2,1)}, bf16[2,8192]{1,0:T(2,128)(2,1)S(1)}, u32[]{:S(2)}, u32[]{:S(2)}) collective-permute-start(bf16[2,8192]{1,0:T(2,128)(2,1)} %refs_0_.1), channel_id=1, source_target_pairs={{0,8},{1,9},{2,10},{3,11},{4,12},{5,13},{6,14},{7,15},{8,0},{9,1},... | collective-permute-start | bytes 98312 | tf_op jit(solution)/shard_map/ppermute | solution.py:408
  4.7 1.5 %collective-permute-start.1 = (bf16[2,8192]{1,0:T(2,128)(2,1)}, bf16[2,8192]{1,0:T(2,128)(2,1)S(1)}, u32[]{:S(2)}, u32[]{:S(2)}) collective-permute-start(bf16[2,8192]{1,0:T(2,128)(2,1)} %refs_1_.1), channel_id=1, source_target_pairs={{0,2},{1,3},{2,0},{3,1},{4,6},{5,7},{6,4},{7,5},{8,10},{9,11},{10,... | collective-permute-start | bytes 98312 | tf_op jit(solution)/shard_map/ppermute | solution.py:408
  6.2 3.0 %enter.1 = (bf16[2,8192]{1,0:T(2,128)(2,1)S(1)}, bf16[2,8192]{1,0:T(2,128)(2,1)S(1)}, s32[3,4,8]{2,1,0:T(4,128)S(4)}, s32[3,8]{1,0:T(4,128)S(4)}, f32[8,4,128,12...) custom-call(bf16[2,8192]{1,0:T(2,128)(2,1)} %refs_0_.1, ...), custom_call_target="tpu_custom_call" | custom-call | tf_op jit(solution)/shard_map/enter/pallas_call | solution.py:117
  9.2 0.0 collective-permute-done
  9.2 0.1 pad_maximum_fusion.4
  9.3 0.0 collective-permute-done.1
  9.3 0.1 pad_maximum_fusion.5
  9.4 0.6 collective-permute-start.3
  10.1 1.9 %collective-permute-start.2 = (bf16[4,8192]{1,0:T(4,128)(2,1)S(1)}, bf16[4,8192]{1,0:T(4,128)(2,1)S(1)}, u32[]{:S(2)}, u32[]{:S(2)}) collective-permute-start(bf16[4,8192]{1,0:T(4,128)(2,1)S(1)} %pad_maximum_fusion.4), channel_id=1, source_target_pairs={{0,4},{1,5},{2,6},{3,7},{4,0},{5,1},{6,2},{7,3},{8,12},{9,13},{10,... | collective-permute-start | bytes 196616 | tf_op jit(solution)/shard_map/ppermute | solution.py:408
  11.9 3.5 %patch.2.gate_0 = bf16[4096,1024]{1,0:T(8,128)(2,1)S(1)} custom-call(s32[3,4,8]{2,1,0:T(4,128)S(4)} %get-tuple-element.89.kept, s32[2,9]{1,0:T(2,128)S(4)} %get-tuple-element.52.begins, s32[2,32]{1,0:T(2,128)S(4)} %get-tuple-element.53.entries, f32[8,4,128,128]{3,2,1,0:T(8,128)S(1)} %get-tuple-element.56.delta, bf16[8192,1024]{1,0:T(8,128)(2,1)} %weight.3), custom_call_target="tpu_custom_call" | custom-call | bytes 8388608 | tf_op jit(solution)/shard_map/patch/pallas_call | solution.py:161
  15.4 0.0 collective-permute-done.3
  15.4 0.1 fusion.3
  15.5 0.2 pad_maximum_fusion.3
  15.7 0.0 collective-permute-done.2
  15.7 0.1 pad_maximum_fusion.2
  15.7 0.8 %collective-permute-start.5 = (bf16[8,8192]{1,0:T(8,128)(2,1)S(1)}, bf16[8,8192]{1,0:T(8,128)(2,1)S(1)}, u32[]{:S(2)}, u32[]{:S(2)}) collective-permute-start(bf16[8,8192]{1,0:T(8,128)(2,1)S(1)} %pad_maximum_fusion.3), channel_id=1, source_target_pairs={{0,4},{1,5},{2,6},{3,7},{4,0},{5,1},{6,2},{7,3},{8,12},{9,13},{10,... | collective-permute-start | bytes 393224 | tf_op jit(solution)/shard_map/ppermute | solution.py:408
  16.6 1.3 %collective-permute-start.4 = (bf16[8,8192]{1,0:T(8,128)(2,1)S(1)}, bf16[8,8192]{1,0:T(8,128)(2,1)S(1)}, u32[]{:S(2)}, u32[]{:S(2)}) collective-permute-start(bf16[8,8192]{1,0:T(8,128)(2,1)S(1)} %pad_maximum_fusion.2), channel_id=1, source_target_pairs={{0,2},{1,3},{2,0},{3,1},{4,6},{5,7},{6,4},{7,5},{8,10},{9,11},{10,... | collective-permute-start | bytes 393224 | tf_op jit(solution)/shard_map/ppermute | solution.py:408
  17.9 3.5 %patch.3.gate_1 = bf16[4096,1024]{1,0:T(8,128)(2,1)S(1)} custom-call(s32[3,4,8]{2,1,0:T(4,128)S(4)} %get-tuple-element.89.kept, s32[2,9]{1,0:T(2,128)S(4)} %get-tuple-element.52.begins, s32[2,32]{1,0:T(2,128)S(4)} %get-tuple-element.53.entries, f32[8,4,128,128]{3,2,1,0:T(8,128)S(1)} %get-tuple-element.56.delta, bf16[8192,1024]{1,0:T(8,128)(2,1)} %weight.3), custom_call_target="tpu_custom_call" | custom-call | bytes 8388608 | tf_op jit(solution)/shard_map/patch/pallas_call | solution.py:161
  21.5 0.0 collective-permute-done.5
  21.5 0.2 pad_maximum_fusion.1.cotangent_0
  21.7 0.0 collective-permute-done.4
  21.7 0.1 collective-permute-start.6
  21.8 0.5 collective-permute-start.7
  22.3 1.0 %collective-permute-done.6.tokens_1 = bf16[16,8192]{1,0:T(8,128)(2,1)S(1)} collective-permute-done((bf16[16,8192]{1,0:T(8,128)(2,1)S(1)}, bf16[16,8192]{1,0:T(8,128)(2,1)S(1)}, u32[]{:S(2)}, u32[]{:S(2)}) %collective-permute-start.6) | collective-permute-done | bytes 262176 | tf_op jit(solution)/shard_map/ppermute | solution.py:408
  23.3 0.4 collective-permute-done.7.cotangent_1
  23.7 23.8 %layer.1 = (f32[16,8192]{1,0:T(8,128)S(1)}, bf16[16,8192]{1,0:T(8,128)(2,1)S(1)}, bf16[32,8192]{1,0:T(8,128)(2,1)S(1)}, bf16[32,8192]{1,0:T(8,128)(2,1)S(1)}, bf...) custom-call(s32[3,4,8]{2,1,0:T(4,128)S(4)} %get-tuple-element.89.kep, ...), custom_call_target="tpu_custom_call" | custom-call | flops 2684354560 | bytes 83886080 | tf_op jit(solution)/shard_map/layer/pallas_call | solution.py:327
  47.5 0.3 collective-permute-start.8
  47.7 1.3 %collective-permute-done.8 = bf16[16,8192]{1,0:T(8,128)(2,1)S(1)} collective-permute-done((bf16[16,8192]{1,0:T(8,128)(2,1)S(1)}, bf16[16,8192]{1,0:T(8,128)(2,1)S(1)}, u32[]{:S(2)}, u32[]{:S(2)}) %collective-permute-start.8) | collective-permute-done | bytes 262176 | tf_op jit(solution)/shard_map/ppermute | solution.py:408
  49.2 1.4 %collective-permute-start.9 = (bf16[8,8192]{1,0:T(8,128)(2,1)S(1)}, bf16[8,8192]{1,0:T(8,128)(2,1)S(1)}, u32[]{:S(2)}, u32[]{:S(2)}) collective-permute-start(bf16[8,8192]{1,0:T(8,128)(2,1)S(1)} %slice.73), channel_id=1, source_target_pairs={{0,2},{1,3},{2,0},{3,1},{4,6},{5,7},{6,4},{7,5},{8,10},{9,11},{10,... | collective-permute-start | bytes 393224 | tf_op jit(solution)/shard_map/ppermute | solution.py:408
  50.5 3.4 %adam.3 = (f32[3,8,4,128,128]{4,3,2,1,0:T(8,128)}, f32[3,8,4,128,128]{4,3,2,1,0:T(8,128)}, f32[3,8,4,128,128]{4,3,2,1,0:T(8,128)}) custom-call(s32[3,4,8]{2,1,0:T(4,128)S(4)} %get-tuple-element.89.kept, s32[3,8]{1,0:T(4,128)S(4)} %get-tuple-element.51.counts, bf16[32,8192]{1,0:T(8,128)(2,1)S(1)} %get-tuple-element.77.left, ...), custom_call_target="tpu_custom_call" | custom-call | bytes 6291456 | tf_op jit(solution)/shard_map/adam/pallas_call | solution.py:394
  54.0 0.8 %collective-permute-done.9 = bf16[8,8192]{1,0:T(8,128)(2,1)S(1)} collective-permute-done((bf16[8,8192]{1,0:T(8,128)(2,1)S(1)}, bf16[8,8192]{1,0:T(8,128)(2,1)S(1)}, u32[]{:S(2)}, u32[]{:S(2)}) %collective-permute-start.9) | collective-permute-done | bytes 131104 | tf_op jit(solution)/shard_map/ppermute | solution.py:408
  54.9 1.7 %collective-permute-start.10 = (bf16[4,8192]{1,0:T(4,128)(2,1)S(1)}, bf16[4,8192]{1,0:T(4,128)(2,1)S(1)}, u32[]{:S(2)}, u32[]{:S(2)}) collective-permute-start(bf16[4,8192]{1,0:T(4,128)(2,1)S(1)} %slice.74), channel_id=1, source_target_pairs={{0,4},{1,5},{2,6},{3,7},{4,0},{5,1},{6,2},{7,3},{8,12},{9,13},{10,... | collective-permute-start | bytes 196616 | tf_op jit(solution)/shard_map/ppermute | solution.py:408
  56.5 3.4 %adam.4 = (f32[3,8,4,128,128]{4,3,2,1,0:T(8,128)}, f32[3,8,4,128,128]{4,3,2,1,0:T(8,128)}, f32[3,8,4,128,128]{4,3,2,1,0:T(8,128)}) custom-call(s32[3,4,8]{2,1,0:T(4,128)S(4)} %get-tuple-element.89.kept, s32[3,8]{1,0:T(4,128)S(4)} %get-tuple-element.51.counts, ...), custom_call_target="tpu_custom_call", output_to_operand_aliasing={{0}: (7, {}), {1}: (8, {}), {2}: (9, {})} | custom-call | bytes 6291456 | tf_op jit(solution)/shard_map/adam/pallas_call | solution.py:394
  60.0 0.0 collective-permute-done.10
  60.1 2.0 %collective-permute-start.11 = (bf16[2,8192]{1,0:T(2,128)(2,1)S(1)}, bf16[2,8192]{1,0:T(2,128)(2,1)S(1)}, u32[]{:S(2)}, u32[]{:S(2)}) collective-permute-start(bf16[2,8192]{1,0:T(2,128)(2,1)S(1)} %slice.75), channel_id=1, source_target_pairs={{0,8},{1,9},{2,10},{3,11},{4,12},{5,13},{6,14},{7,15},{8,0},{9,1},... | collective-permute-start | bytes 98312 | tf_op jit(solution)/shard_map/ppermute | solution.py:408
  62.1 3.4 %adam.5 = (f32[3,8,4,128,128]{4,3,2,1,0:T(8,128)}, f32[3,8,4,128,128]{4,3,2,1,0:T(8,128)}, f32[3,8,4,128,128]{4,3,2,1,0:T(8,128)}) custom-call(s32[3,4,8]{2,1,0:T(4,128)S(4)} %get-tuple-element.89.kept, s32[3,8]{1,0:T(4,128)S(4)} %get-tuple-element.51.counts, ...), custom_call_target="tpu_custom_call", output_to_operand_aliasing={{0}: (7, {}), {1}: (8, {}), {2}: (9, {})} | custom-call | bytes 6291456 | tf_op jit(solution)/shard_map/adam/pallas_call | solution.py:394
  65.5 0.0 collective-permute-done.11
  65.5 0.7 convert_add_fusion.2
  (10 shorter events, 0.4 us)
Async XLA Ops:
  0.6 8.6 %collective-permute-start = (bf16[2,8192]{1,0:T(2,128)(2,1)}, bf16[2,8192]{1,0:T(2,128)(2,1)S(1)}, u32[]{:S(2)}, u32[]{:S(2)}) collective-permute-start(bf16[2,8192]{1,0:T(2,128)(2,1)} %refs_0_.1), channel_id=1, source_target_pairs={{0,8},{1,9},{2,10},{3,11},{4,12},{5,13},{6,14},{7,15},{8,0},{9,1},... | collective-permute-start | bytes 98312 | tf_op jit(solution)/shard_map/ppermute | solution.py:408
  4.7 4.5 %collective-permute-start.1 = (bf16[2,8192]{1,0:T(2,128)(2,1)}, bf16[2,8192]{1,0:T(2,128)(2,1)S(1)}, u32[]{:S(2)}, u32[]{:S(2)}) collective-permute-start(bf16[2,8192]{1,0:T(2,128)(2,1)} %refs_1_.1), channel_id=1, source_target_pairs={{0,2},{1,3},{2,0},{3,1},{4,6},{5,7},{6,4},{7,5},{8,10},{9,11},{10,... | collective-permute-start | bytes 98312 | tf_op jit(solution)/shard_map/ppermute | solution.py:408
  9.4 6.1 %collective-permute-start.3 = (bf16[4,8192]{1,0:T(4,128)(2,1)S(1)}, bf16[4,8192]{1,0:T(4,128)(2,1)S(1)}, u32[]{:S(2)}, u32[]{:S(2)}) collective-permute-start(bf16[4,8192]{1,0:T(4,128)(2,1)S(1)} %pad_maximum_fusion.5), channel_id=1, source_target_pairs={{0,8},{1,9},{2,10},{3,11},{4,12},{5,13},{6,14},{7,15},{8,0},{9,1},... | collective-permute-start | bytes 196616 | tf_op jit(solution)/shard_map/ppermute | solution.py:408
  10.1 5.6 %collective-permute-start.2 = (bf16[4,8192]{1,0:T(4,128)(2,1)S(1)}, bf16[4,8192]{1,0:T(4,128)(2,1)S(1)}, u32[]{:S(2)}, u32[]{:S(2)}) collective-permute-start(bf16[4,8192]{1,0:T(4,128)(2,1)S(1)} %pad_maximum_fusion.4), channel_id=1, source_target_pairs={{0,4},{1,5},{2,6},{3,7},{4,0},{5,1},{6,2},{7,3},{8,12},{9,13},{10,... | collective-permute-start | bytes 196616 | tf_op jit(solution)/shard_map/ppermute | solution.py:408
  15.7 5.7 %collective-permute-start.5 = (bf16[8,8192]{1,0:T(8,128)(2,1)S(1)}, bf16[8,8192]{1,0:T(8,128)(2,1)S(1)}, u32[]{:S(2)}, u32[]{:S(2)}) collective-permute-start(bf16[8,8192]{1,0:T(8,128)(2,1)S(1)} %pad_maximum_fusion.3), channel_id=1, source_target_pairs={{0,4},{1,5},{2,6},{3,7},{4,0},{5,1},{6,2},{7,3},{8,12},{9,13},{10,... | collective-permute-start | bytes 393224 | tf_op jit(solution)/shard_map/ppermute | solution.py:408
  16.6 5.1 %collective-permute-start.4 = (bf16[8,8192]{1,0:T(8,128)(2,1)S(1)}, bf16[8,8192]{1,0:T(8,128)(2,1)S(1)}, u32[]{:S(2)}, u32[]{:S(2)}) collective-permute-start(bf16[8,8192]{1,0:T(8,128)(2,1)S(1)} %pad_maximum_fusion.2), channel_id=1, source_target_pairs={{0,2},{1,3},{2,0},{3,1},{4,6},{5,7},{6,4},{7,5},{8,10},{9,11},{10,... | collective-permute-start | bytes 393224 | tf_op jit(solution)/shard_map/ppermute | solution.py:408
  21.7 1.6 %collective-permute-start.6 = (bf16[16,8192]{1,0:T(8,128)(2,1)S(1)}, bf16[16,8192]{1,0:T(8,128)(2,1)S(1)}, u32[]{:S(2)}, u32[]{:S(2)}) collective-permute-start(bf16[16,8192]{1,0:T(8,128)(2,1)S(1)} %pad_maximum_fusion.tokens_0), channel_id=1, source_target_pairs={{0,1},{1,0},{2,3},{3,2},{4,5},{5,4},{6,7},{7,6},{8,9},{9,8},{10,11... | collective-permute-start | bytes 786440 | tf_op jit(solution)/shard_map/ppermute | solution.py:408
  21.8 1.9 %collective-permute-start.7 = (bf16[16,8192]{1,0:T(8,128)(2,1)S(1)}, bf16[16,8192]{1,0:T(8,128)(2,1)S(1)}, u32[]{:S(2)}, u32[]{:S(2)}) collective-permute-start(bf16[16,8192]{1,0:T(8,128)(2,1)S(1)} %pad_maximum_fusion.1.cotangent_0), channel_id=1, source_target_pairs={{0,1},{1,0},{2,3},{3,2},{4,5},{5,4},{6,7},{7,6},{8,9},{9,8},{10,11... | collective-permute-start | bytes 786440 | tf_op jit(solution)/shard_map/ppermute | solution.py:408
  47.5 1.6 %collective-permute-start.8 = (bf16[16,8192]{1,0:T(8,128)(2,1)S(1)}, bf16[16,8192]{1,0:T(8,128)(2,1)S(1)}, u32[]{:S(2)}, u32[]{:S(2)}) collective-permute-start(bf16[16,8192]{1,0:T(8,128)(2,1)S(1)} %get-tuple-element.68), channel_id=1, source_target_pairs={{0,1},{1,0},{2,3},{3,2},{4,5},{5,4},{6,7},{7,6},{8,9},{9,8},{10,11... | collective-permute-start | bytes 786440 | tf_op jit(solution)/shard_map/ppermute | solution.py:408
  49.2 5.7 %collective-permute-start.9 = (bf16[8,8192]{1,0:T(8,128)(2,1)S(1)}, bf16[8,8192]{1,0:T(8,128)(2,1)S(1)}, u32[]{:S(2)}, u32[]{:S(2)}) collective-permute-start(bf16[8,8192]{1,0:T(8,128)(2,1)S(1)} %slice.73), channel_id=1, source_target_pairs={{0,2},{1,3},{2,0},{3,1},{4,6},{5,7},{6,4},{7,5},{8,10},{9,11},{10,... | collective-permute-start | bytes 393224 | tf_op jit(solution)/shard_map/ppermute | solution.py:408
  54.9 5.1 %collective-permute-start.10 = (bf16[4,8192]{1,0:T(4,128)(2,1)S(1)}, bf16[4,8192]{1,0:T(4,128)(2,1)S(1)}, u32[]{:S(2)}, u32[]{:S(2)}) collective-permute-start(bf16[4,8192]{1,0:T(4,128)(2,1)S(1)} %slice.74), channel_id=1, source_target_pairs={{0,4},{1,5},{2,6},{3,7},{4,0},{5,1},{6,2},{7,3},{8,12},{9,13},{10,... | collective-permute-start | bytes 196616 | tf_op jit(solution)/shard_map/ppermute | solution.py:408
  60.1 5.4 %collective-permute-start.11 = (bf16[2,8192]{1,0:T(2,128)(2,1)S(1)}, bf16[2,8192]{1,0:T(2,128)(2,1)S(1)}, u32[]{:S(2)}, u32[]{:S(2)}) collective-permute-start(bf16[2,8192]{1,0:T(2,128)(2,1)S(1)} %slice.75), channel_id=1, source_target_pairs={{0,8},{1,9},{2,10},{3,11},{4,12},{5,13},{6,14},{7,15},{8,0},{9,1},... | collective-permute-start | bytes 98312 | tf_op jit(solution)/shard_map/ppermute | solution.py:408

commit v4 on v3

--- a/solution.py
+++ b/solution.py
@@ -382,7 +382,7 @@
             write(a, t).start()
         return carry
 
-    lax.fori_loop(0, tiles, tile, 0, unroll=min(tiles, 2))
+    lax.fori_loop(0, tiles, tile, 0, unroll=min(tiles, 4))
     for t in range(tiles):
         for a in range(3):
             write(a, t).wait()

time: 66.3 us -> 65.9 us (level)
  transfers between devices with their start and end apart: 12 -> 12, of which waited for: 4 -> 4; matrix products, arithmetic and copies ran while one was open for 1% -> 1% of each run, Pallas kernels for 31% -> 30%
where the time goes in v4:
time: 65.9 us; the launch traced here: 65.8 us
  Pallas kernels  43.7 us (66%)
  starting transfers between devices  15.5 us (24%)
  waiting for transfers between devices  4.14 us (6%)
  other arithmetic  1.32 us (2%)
  between operations  0.86 us (1%)
    pallas_call x1, Pallas kernels, layer(): pl.pallas_call(functools.partial(layer_kernel, wide, step), out_shape=(pl...  23.9 us
    ppermute x12, starting transfers between devices, exchange(): return lax.ppermute(value, 'dp', [(i, i ^ distance) for i in range(size)])  15.5 us
    pallas_call x3, Pallas kernels, adam(): pl.pallas_call(functools.partial(adam_kernel, which), out_shape=(out, out...  9.73 us
    pallas_call x2, Pallas kernels, patched(): pl.pallas_call(functools.partial(patch_kernel, which, offset, step), out_...  7.13 us
    ppermute x12, waiting for transfers between devices, exchange(): return lax.ppermute(value, 'dp', [(i, i ^ distance) for i in range(size)])  4.14 us
    pallas_call x1, Pallas kernels, into_vmem(): pl.pallas_call(functools.partial(enter_kernel, per_part, len(whole)), out...  2.95 us
  transfers between devices with their start and end apart: 12, of which 4 were waited for; matrix products, arithmetic and copies ran while one was open for 1% of the time, Pallas kernels for 30%

profile of v4, /device:TPU:0, one launch (start us, length us, event | category | flops | bytes accessed | tf_op | source)
XLA Modules:
  0.0 65.8 jit_solution(9378973049705381508)
XLA Ops:
  0.6 4.1 %collective-permute-start = (bf16[2,8192]{1,0:T(2,128)(2,1)}, bf16[2,8192]{1,0:T(2,128)(2,1)S(1)}, u32[]{:S(2)}, u32[]{:S(2)}) collective-permute-start(bf16[2,8192]{1,0:T(2,128)(2,1)} %refs_0_.1), channel_id=1, source_target_pairs={{0,8},{1,9},{2,10},{3,11},{4,12},{5,13},{6,14},{7,15},{8,0},{9,1},... | collective-permute-start | bytes 98312 | tf_op jit(solution)/shard_map/ppermute | solution.py:408
  4.7 1.5 %collective-permute-start.1 = (bf16[2,8192]{1,0:T(2,128)(2,1)}, bf16[2,8192]{1,0:T(2,128)(2,1)S(1)}, u32[]{:S(2)}, u32[]{:S(2)}) collective-permute-start(bf16[2,8192]{1,0:T(2,128)(2,1)} %refs_1_.1), channel_id=1, source_target_pairs={{0,2},{1,3},{2,0},{3,1},{4,6},{5,7},{6,4},{7,5},{8,10},{9,11},{10,... | collective-permute-start | bytes 98312 | tf_op jit(solution)/shard_map/ppermute | solution.py:408
  6.2 3.0 %enter.1 = (bf16[2,8192]{1,0:T(2,128)(2,1)S(1)}, bf16[2,8192]{1,0:T(2,128)(2,1)S(1)}, s32[3,4,8]{2,1,0:T(4,128)S(4)}, s32[3,8]{1,0:T(4,128)S(4)}, f32[8,4,128,12...) custom-call(bf16[2,8192]{1,0:T(2,128)(2,1)} %refs_0_.1, ...), custom_call_target="tpu_custom_call" | custom-call | tf_op jit(solution)/shard_map/enter/pallas_call | solution.py:117
  9.2 0.0 collective-permute-done
  9.2 0.1 pad_maximum_fusion.4
  9.3 0.0 collective-permute-done.1
  9.3 0.1 pad_maximum_fusion.5
  9.4 0.6 collective-permute-start.3
  10.1 1.9 %collective-permute-start.2 = (bf16[4,8192]{1,0:T(4,128)(2,1)S(1)}, bf16[4,8192]{1,0:T(4,128)(2,1)S(1)}, u32[]{:S(2)}, u32[]{:S(2)}) collective-permute-start(bf16[4,8192]{1,0:T(4,128)(2,1)S(1)} %pad_maximum_fusion.4), channel_id=1, source_target_pairs={{0,4},{1,5},{2,6},{3,7},{4,0},{5,1},{6,2},{7,3},{8,12},{9,13},{10,... | collective-permute-start | bytes 196616 | tf_op jit(solution)/shard_map/ppermute | solution.py:408
  11.9 3.5 %patch.2.gate_0 = bf16[4096,1024]{1,0:T(8,128)(2,1)S(1)} custom-call(s32[3,4,8]{2,1,0:T(4,128)S(4)} %get-tuple-element.89.kept, s32[2,9]{1,0:T(2,128)S(4)} %get-tuple-element.52.begins, s32[2,32]{1,0:T(2,128)S(4)} %get-tuple-element.53.entries, f32[8,4,128,128]{3,2,1,0:T(8,128)S(1)} %get-tuple-element.56.delta, bf16[8192,1024]{1,0:T(8,128)(2,1)} %weight.3), custom_call_target="tpu_custom_call" | custom-call | bytes 8388608 | tf_op jit(solution)/shard_map/patch/pallas_call | solution.py:161
  15.4 0.0 collective-permute-done.3
  15.5 0.1 fusion.3
  15.5 0.2 pad_maximum_fusion.3
  15.7 0.0 collective-permute-done.2
  15.7 0.1 pad_maximum_fusion.2
  15.8 0.8 %collective-permute-start.5 = (bf16[8,8192]{1,0:T(8,128)(2,1)S(1)}, bf16[8,8192]{1,0:T(8,128)(2,1)S(1)}, u32[]{:S(2)}, u32[]{:S(2)}) collective-permute-start(bf16[8,8192]{1,0:T(8,128)(2,1)S(1)} %pad_maximum_fusion.3), channel_id=1, source_target_pairs={{0,4},{1,5},{2,6},{3,7},{4,0},{5,1},{6,2},{7,3},{8,12},{9,13},{10,... | collective-permute-start | bytes 393224 | tf_op jit(solution)/shard_map/ppermute | solution.py:408
  16.6 1.3 %collective-permute-start.4 = (bf16[8,8192]{1,0:T(8,128)(2,1)S(1)}, bf16[8,8192]{1,0:T(8,128)(2,1)S(1)}, u32[]{:S(2)}, u32[]{:S(2)}) collective-permute-start(bf16[8,8192]{1,0:T(8,128)(2,1)S(1)} %pad_maximum_fusion.2), channel_id=1, source_target_pairs={{0,2},{1,3},{2,0},{3,1},{4,6},{5,7},{6,4},{7,5},{8,10},{9,11},{10,... | collective-permute-start | bytes 393224 | tf_op jit(solution)/shard_map/ppermute | solution.py:408
  17.9 3.6 %patch.3.gate_1 = bf16[4096,1024]{1,0:T(8,128)(2,1)S(1)} custom-call(s32[3,4,8]{2,1,0:T(4,128)S(4)} %get-tuple-element.89.kept, s32[2,9]{1,0:T(2,128)S(4)} %get-tuple-element.52.begins, s32[2,32]{1,0:T(2,128)S(4)} %get-tuple-element.53.entries, f32[8,4,128,128]{3,2,1,0:T(8,128)S(1)} %get-tuple-element.56.delta, bf16[8192,1024]{1,0:T(8,128)(2,1)} %weight.3), custom_call_target="tpu_custom_call" | custom-call | bytes 8388608 | tf_op jit(solution)/shard_map/patch/pallas_call | solution.py:161
  21.6 0.0 collective-permute-done.5
  21.6 0.2 pad_maximum_fusion.1.cotangent_0
  21.8 0.0 collective-permute-done.4
  21.8 0.1 collective-permute-start.6
  21.9 0.5 collective-permute-start.7
  22.4 1.0 %collective-permute-done.6.tokens_1 = bf16[16,8192]{1,0:T(8,128)(2,1)S(1)} collective-permute-done((bf16[16,8192]{1,0:T(8,128)(2,1)S(1)}, bf16[16,8192]{1,0:T(8,128)(2,1)S(1)}, u32[]{:S(2)}, u32[]{:S(2)}) %collective-permute-start.6) | collective-permute-done | bytes 262176 | tf_op jit(solution)/shard_map/ppermute | solution.py:408
  23.4 0.4 collective-permute-done.7.cotangent_1
  23.8 23.9 %layer.1 = (f32[16,8192]{1,0:T(8,128)S(1)}, bf16[16,8192]{1,0:T(8,128)(2,1)S(1)}, bf16[32,8192]{1,0:T(8,128)(2,1)S(1)}, bf16[32,8192]{1,0:T(8,128)(2,1)S(1)}, bf...) custom-call(s32[3,4,8]{2,1,0:T(4,128)S(4)} %get-tuple-element.89.kep, ...), custom_call_target="tpu_custom_call" | custom-call | flops 2684354560 | bytes 83886080 | tf_op jit(solution)/shard_map/layer/pallas_call | solution.py:327
  47.7 0.1 collective-permute-start.8
  47.8 1.5 %collective-permute-done.8 = bf16[16,8192]{1,0:T(8,128)(2,1)S(1)} collective-permute-done((bf16[16,8192]{1,0:T(8,128)(2,1)S(1)}, bf16[16,8192]{1,0:T(8,128)(2,1)S(1)}, u32[]{:S(2)}, u32[]{:S(2)}) %collective-permute-start.8) | collective-permute-done | bytes 262176 | tf_op jit(solution)/shard_map/ppermute | solution.py:408
  49.4 1.2 %collective-permute-start.9 = (bf16[8,8192]{1,0:T(8,128)(2,1)S(1)}, bf16[8,8192]{1,0:T(8,128)(2,1)S(1)}, u32[]{:S(2)}, u32[]{:S(2)}) collective-permute-start(bf16[8,8192]{1,0:T(8,128)(2,1)S(1)} %slice.73), channel_id=1, source_target_pairs={{0,2},{1,3},{2,0},{3,1},{4,6},{5,7},{6,4},{7,5},{8,10},{9,11},{10,... | collective-permute-start | bytes 393224 | tf_op jit(solution)/shard_map/ppermute | solution.py:408
  50.5 3.2 %adam.3 = (f32[3,8,4,128,128]{4,3,2,1,0:T(8,128)}, f32[3,8,4,128,128]{4,3,2,1,0:T(8,128)}, f32[3,8,4,128,128]{4,3,2,1,0:T(8,128)}) custom-call(s32[3,4,8]{2,1,0:T(4,128)S(4)} %get-tuple-element.89.kept, s32[3,8]{1,0:T(4,128)S(4)} %get-tuple-element.51.counts, bf16[32,8192]{1,0:T(8,128)(2,1)S(1)} %get-tuple-element.77.left, ...), custom_call_target="tpu_custom_call" | custom-call | bytes 6291456 | tf_op jit(solution)/shard_map/adam/pallas_call | solution.py:394
  53.8 1.2 %collective-permute-done.9 = bf16[8,8192]{1,0:T(8,128)(2,1)S(1)} collective-permute-done((bf16[8,8192]{1,0:T(8,128)(2,1)S(1)}, bf16[8,8192]{1,0:T(8,128)(2,1)S(1)}, u32[]{:S(2)}, u32[]{:S(2)}) %collective-permute-start.9) | collective-permute-done | bytes 131104 | tf_op jit(solution)/shard_map/ppermute | solution.py:408
  55.1 1.6 %collective-permute-start.10 = (bf16[4,8192]{1,0:T(4,128)(2,1)S(1)}, bf16[4,8192]{1,0:T(4,128)(2,1)S(1)}, u32[]{:S(2)}, u32[]{:S(2)}) collective-permute-start(bf16[4,8192]{1,0:T(4,128)(2,1)S(1)} %slice.74), channel_id=1, source_target_pairs={{0,4},{1,5},{2,6},{3,7},{4,0},{5,1},{6,2},{7,3},{8,12},{9,13},{10,... | collective-permute-start | bytes 196616 | tf_op jit(solution)/shard_map/ppermute | solution.py:408
  56.6 3.2 %adam.4 = (f32[3,8,4,128,128]{4,3,2,1,0:T(8,128)}, f32[3,8,4,128,128]{4,3,2,1,0:T(8,128)}, f32[3,8,4,128,128]{4,3,2,1,0:T(8,128)}) custom-call(s32[3,4,8]{2,1,0:T(4,128)S(4)} %get-tuple-element.89.kept, s32[3,8]{1,0:T(4,128)S(4)} %get-tuple-element.51.counts, ...), custom_call_target="tpu_custom_call", output_to_operand_aliasing={{0}: (7, {}), {1}: (8, {}), {2}: (9, {})} | custom-call | bytes 6291456 | tf_op jit(solution)/shard_map/adam/pallas_call | solution.py:394
  59.9 0.0 collective-permute-done.10
  60.0 1.9 %collective-permute-start.11 = (bf16[2,8192]{1,0:T(2,128)(2,1)S(1)}, bf16[2,8192]{1,0:T(2,128)(2,1)S(1)}, u32[]{:S(2)}, u32[]{:S(2)}) collective-permute-start(bf16[2,8192]{1,0:T(2,128)(2,1)S(1)} %slice.75), channel_id=1, source_target_pairs={{0,8},{1,9},{2,10},{3,11},{4,12},{5,13},{6,14},{7,15},{8,0},{9,1},... | collective-permute-start | bytes 98312 | tf_op jit(solution)/shard_map/ppermute | solution.py:408
  61.9 3.3 %adam.5 = (f32[3,8,4,128,128]{4,3,2,1,0:T(8,128)}, f32[3,8,4,128,128]{4,3,2,1,0:T(8,128)}, f32[3,8,4,128,128]{4,3,2,1,0:T(8,128)}) custom-call(s32[3,4,8]{2,1,0:T(4,128)S(4)} %get-tuple-element.89.kept, s32[3,8]{1,0:T(4,128)S(4)} %get-tuple-element.51.counts, ...), custom_call_target="tpu_custom_call", output_to_operand_aliasing={{0}: (7, {}), {1}: (8, {}), {2}: (9, {})} | custom-call | bytes 6291456 | tf_op jit(solution)/shard_map/adam/pallas_call | solution.py:394
  65.1 0.0 collective-permute-done.11
  65.1 0.7 convert_add_fusion.2
  (10 shorter events, 0.4 us)
Async XLA Ops:
  0.6 8.6 %collective-permute-start = (bf16[2,8192]{1,0:T(2,128)(2,1)}, bf16[2,8192]{1,0:T(2,128)(2,1)S(1)}, u32[]{:S(2)}, u32[]{:S(2)}) collective-permute-start(bf16[2,8192]{1,0:T(2,128)(2,1)} %refs_0_.1), channel_id=1, source_target_pairs={{0,8},{1,9},{2,10},{3,11},{4,12},{5,13},{6,14},{7,15},{8,0},{9,1},... | collective-permute-start | bytes 98312 | tf_op jit(solution)/shard_map/ppermute | solution.py:408
  4.7 4.5 %collective-permute-start.1 = (bf16[2,8192]{1,0:T(2,128)(2,1)}, bf16[2,8192]{1,0:T(2,128)(2,1)S(1)}, u32[]{:S(2)}, u32[]{:S(2)}) collective-permute-start(bf16[2,8192]{1,0:T(2,128)(2,1)} %refs_1_.1), channel_id=1, source_target_pairs={{0,2},{1,3},{2,0},{3,1},{4,6},{5,7},{6,4},{7,5},{8,10},{9,11},{10,... | collective-permute-start | bytes 98312 | tf_op jit(solution)/shard_map/ppermute | solution.py:408
  9.4 6.1 %collective-permute-start.3 = (bf16[4,8192]{1,0:T(4,128)(2,1)S(1)}, bf16[4,8192]{1,0:T(4,128)(2,1)S(1)}, u32[]{:S(2)}, u32[]{:S(2)}) collective-permute-start(bf16[4,8192]{1,0:T(4,128)(2,1)S(1)} %pad_maximum_fusion.5), channel_id=1, source_target_pairs={{0,8},{1,9},{2,10},{3,11},{4,12},{5,13},{6,14},{7,15},{8,0},{9,1},... | collective-permute-start | bytes 196616 | tf_op jit(solution)/shard_map/ppermute | solution.py:408
  10.1 5.6 %collective-permute-start.2 = (bf16[4,8192]{1,0:T(4,128)(2,1)S(1)}, bf16[4,8192]{1,0:T(4,128)(2,1)S(1)}, u32[]{:S(2)}, u32[]{:S(2)}) collective-permute-start(bf16[4,8192]{1,0:T(4,128)(2,1)S(1)} %pad_maximum_fusion.4), channel_id=1, source_target_pairs={{0,4},{1,5},{2,6},{3,7},{4,0},{5,1},{6,2},{7,3},{8,12},{9,13},{10,... | collective-permute-start | bytes 196616 | tf_op jit(solution)/shard_map/ppermute | solution.py:408
  15.8 5.8 %collective-permute-start.5 = (bf16[8,8192]{1,0:T(8,128)(2,1)S(1)}, bf16[8,8192]{1,0:T(8,128)(2,1)S(1)}, u32[]{:S(2)}, u32[]{:S(2)}) collective-permute-start(bf16[8,8192]{1,0:T(8,128)(2,1)S(1)} %pad_maximum_fusion.3), channel_id=1, source_target_pairs={{0,4},{1,5},{2,6},{3,7},{4,0},{5,1},{6,2},{7,3},{8,12},{9,13},{10,... | collective-permute-start | bytes 393224 | tf_op jit(solution)/shard_map/ppermute | solution.py:408
  16.6 5.2 %collective-permute-start.4 = (bf16[8,8192]{1,0:T(8,128)(2,1)S(1)}, bf16[8,8192]{1,0:T(8,128)(2,1)S(1)}, u32[]{:S(2)}, u32[]{:S(2)}) collective-permute-start(bf16[8,8192]{1,0:T(8,128)(2,1)S(1)} %pad_maximum_fusion.2), channel_id=1, source_target_pairs={{0,2},{1,3},{2,0},{3,1},{4,6},{5,7},{6,4},{7,5},{8,10},{9,11},{10,... | collective-permute-start | bytes 393224 | tf_op jit(solution)/shard_map/ppermute | solution.py:408
  21.8 1.6 %collective-permute-start.6 = (bf16[16,8192]{1,0:T(8,128)(2,1)S(1)}, bf16[16,8192]{1,0:T(8,128)(2,1)S(1)}, u32[]{:S(2)}, u32[]{:S(2)}) collective-permute-start(bf16[16,8192]{1,0:T(8,128)(2,1)S(1)} %pad_maximum_fusion.tokens_0), channel_id=1, source_target_pairs={{0,1},{1,0},{2,3},{3,2},{4,5},{5,4},{6,7},{7,6},{8,9},{9,8},{10,11... | collective-permute-start | bytes 786440 | tf_op jit(solution)/shard_map/ppermute | solution.py:408
  21.9 1.9 %collective-permute-start.7 = (bf16[16,8192]{1,0:T(8,128)(2,1)S(1)}, bf16[16,8192]{1,0:T(8,128)(2,1)S(1)}, u32[]{:S(2)}, u32[]{:S(2)}) collective-permute-start(bf16[16,8192]{1,0:T(8,128)(2,1)S(1)} %pad_maximum_fusion.1.cotangent_0), channel_id=1, source_target_pairs={{0,1},{1,0},{2,3},{3,2},{4,5},{5,4},{6,7},{7,6},{8,9},{9,8},{10,11... | collective-permute-start | bytes 786440 | tf_op jit(solution)/shard_map/ppermute | solution.py:408
  47.7 1.6 %collective-permute-start.8 = (bf16[16,8192]{1,0:T(8,128)(2,1)S(1)}, bf16[16,8192]{1,0:T(8,128)(2,1)S(1)}, u32[]{:S(2)}, u32[]{:S(2)}) collective-permute-start(bf16[16,8192]{1,0:T(8,128)(2,1)S(1)} %get-tuple-element.68), channel_id=1, source_target_pairs={{0,1},{1,0},{2,3},{3,2},{4,5},{5,4},{6,7},{7,6},{8,9},{9,8},{10,11... | collective-permute-start | bytes 786440 | tf_op jit(solution)/shard_map/ppermute | solution.py:408
  49.4 5.6 %collective-permute-start.9 = (bf16[8,8192]{1,0:T(8,128)(2,1)S(1)}, bf16[8,8192]{1,0:T(8,128)(2,1)S(1)}, u32[]{:S(2)}, u32[]{:S(2)}) collective-permute-start(bf16[8,8192]{1,0:T(8,128)(2,1)S(1)} %slice.73), channel_id=1, source_target_pairs={{0,2},{1,3},{2,0},{3,1},{4,6},{5,7},{6,4},{7,5},{8,10},{9,11},{10,... | collective-permute-start | bytes 393224 | tf_op jit(solution)/shard_map/ppermute | solution.py:408
  55.1 4.8 %collective-permute-start.10 = (bf16[4,8192]{1,0:T(4,128)(2,1)S(1)}, bf16[4,8192]{1,0:T(4,128)(2,1)S(1)}, u32[]{:S(2)}, u32[]{:S(2)}) collective-permute-start(bf16[4,8192]{1,0:T(4,128)(2,1)S(1)} %slice.74), channel_id=1, source_target_pairs={{0,4},{1,5},{2,6},{3,7},{4,0},{5,1},{6,2},{7,3},{8,12},{9,13},{10,... | collective-permute-start | bytes 196616 | tf_op jit(solution)/shard_map/ppermute | solution.py:408
  60.0 5.1 %collective-permute-start.11 = (bf16[2,8192]{1,0:T(2,128)(2,1)S(1)}, bf16[2,8192]{1,0:T(2,128)(2,1)S(1)}, u32[]{:S(2)}, u32[]{:S(2)}) collective-permute-start(bf16[2,8192]{1,0:T(2,128)(2,1)S(1)} %slice.75), channel_id=1, source_target_pairs={{0,8},{1,9},{2,10},{3,11},{4,12},{5,13},{6,14},{7,15},{8,0},{9,1},... | collective-permute-start | bytes 98312 | tf_op jit(solution)/shard_map/ppermute | solution.py:408

commit v5 on v4

--- a/solution.py
+++ b/solution.py
@@ -356,52 +356,80 @@
     )
 
 
-def adam_kernel(which, kept, counts, left, right, delta, first, second, *refs):
+def adam_kernel(ranges, kept, counts, hidden, gate_grad, up_grad, tokens, cotangent, *refs):
+    used = len({which for which, _, _ in ranges})
+    deltas, firsts, seconds = refs[:used], refs[used : 2 * used], refs[2 * used : 3 * used]
     outs = refs[-5:-2]
     made, sems = refs[-2:]
-    tiles, slots, side = delta.shape[:3]
-
-    def write(a, t):
-        return pltpu.make_async_copy(made.at[a, t], outs[a].at[which, t], sems.at[a, t])
-
-    def tile(t, carry):
-        own = chunk(t, side)
-        for k in range(slots):
-            block = chunk(kept[which, k, t], side)
-            if which == 2:
-                grad = dot_cols(left[:, own], right[:, block])
-            else:
-                grad = dot_cols(left[:, block], right[:, own])
-            live = k < counts[which, t]
-            m1 = 0.9 * first[t, k] + 0.1 * grad
-            m2 = 0.999 * second[t, k] + 0.001 * grad * grad
-            value = delta[t, k] - 0.01 * m1 / (jnp.sqrt(m2) + 1e-08)
-            for a, new in enumerate((value, m1, m2)):
-                made[a, t, k] = jnp.where(live, new, 0.0)
+    slots, side = made.shape[2:4]
+    order = []
+
+    for i, (which, begin, end) in enumerate(ranges):
+        delta, first, second = deltas[i], firsts[i], seconds[i]
+        base = len(order)
+
+        def write(a, t, place, which=which):
+            return pltpu.make_async_copy(made.at[a, place], outs[a].at[which, t], sems.at[a, place])
+
+        def tile(t, carry):
+            place = base + t - begin
+            own = chunk(t, side)
+            for k in range(slots):
+                block = chunk(kept[which, k, t], side)
+                if which == 2:
+                    grad = dot_cols(hidden[:, own], cotangent[:, block])
+                else:
+                    grad = dot_cols(tokens[:, block], (gate_grad, up_grad)[which][:, own])
+                live = k < counts[which, t]
+                m1 = 0.9 * first[t, k] + 0.1 * grad
+                m2 = 0.999 * second[t, k] + 0.001 * grad * grad
+                value = delta[t, k] - 0.01 * m1 / (jnp.sqrt(m2) + 1e-08)
+                for a, new in enumerate((value, m1, m2)):
+                    made[a, place, k] = jnp.where(live, new, 0.0)
+            for a in range(3):
+                write(a, t, place).start()
+            return carry
+
+        count = end - begin
+        lax.fori_loop(begin, end, tile, 0, unroll=4 if count % 4 == 0 else 2 if count % 2 == 0 else 1)
+        order += [(write, t, base + t - begin) for t in range(begin, end)]
+    for write, t, place in order:
         for a in range(3):
-            write(a, t).start()
-        return carry
-
-    lax.fori_loop(0, tiles, tile, 0, unroll=min(tiles, 4))
-    for t in range(tiles):
-        for a in range(3):
-            write(a, t).wait()
-
-
-def adam(which, kept, counts, left, right, delta, moment_pair, done):
-    shape = (3, *delta.shape)
-    out = pltpu.HBM(shape, F32)
+            write(a, t, place).wait()
+
+
+def adam(ranges, kept, counts, operands, deltas, fetched, done):
+    blocks = deltas[0].shape
+    tiles = sum(end - begin for _, begin, end in ranges)
+    inputs = [
+        *operands,
+        *(deltas[which] for which, _, _ in ranges),
+        *(fetched[2 * which] for which, _, _ in ranges),
+        *(fetched[2 * which + 1] for which, _, _ in ranges),
+    ]
+    out = pltpu.HBM((3, *blocks), F32)
     return pl.pallas_call(
-        functools.partial(adam_kernel, which),
+        functools.partial(adam_kernel, ranges),
         out_shape=(out, out, out),
-        in_specs=[SMEM_SPEC] * 2 + [VMEM_SPEC] * 5 + [HBM_SPEC] * len(done),
+        in_specs=[SMEM_SPEC] * 2 + [VMEM_SPEC] * len(inputs) + [HBM_SPEC] * len(done),
         out_specs=(HBM_SPEC,) * 3,
-        scratch_shapes=[pltpu.VMEM((3, *shape[1:]), F32), pltpu.SemaphoreType.DMA((3, shape[1]))],
-        input_output_aliases={7 + i: i for i in range(len(done))},
-        compiler_params=params(8 * MIB),
-        cost_estimate=cost(0, 12 * delta.size),
+        scratch_shapes=[pltpu.VMEM((3, tiles, *blocks[1:]), F32), pltpu.SemaphoreType.DMA((3, tiles))],
+        input_output_aliases={2 + len(inputs) + i: i for i in range(len(done))},
+        compiler_params=params(11 * MIB),
+        cost_estimate=cost(0, 12 * tiles * deltas[0][0].size),
         name="adam",
-    )(*in_smem(kept, counts), *in_vmem(left, right, delta, *moment_pair), *in_hbm(*done))
+    )(*in_smem(kept, counts), *in_vmem(*inputs), *in_hbm(*done))
+
+
+def adam_pieces(tiles):
+    cut = tiles // 4
+    pieces = (
+        ((2, 0, cut),),
+        ((0, 0, tiles), (1, 0, cut)),
+        ((1, cut, tiles),),
+        ((2, cut, tiles),),
+    )
+    return [tuple(r for r in ranges if r[1] < r[2]) for ranges in pieces]
 
 
 def exchange(value, distance, size):
@@ -460,23 +488,20 @@
     total, away, tokens, cotangent, hidden, gate_grad, up_grad, *fetched = layer(
         ahead, kept, counts, lists, tokens, cotangent, gate_eff, deltas, up_weight, down_weight, first_moment, second_moment
     )
-    operands = ((tokens, gate_grad), (tokens, up_grad), (hidden, cotangent))
+    operands = (hidden, gate_grad, up_grad, tokens, cotangent)
+    pieces = adam_pieces(sparse_delta.shape[1])
     news = ()
     for i, distance in enumerate(order[::-1]):
         if i:
             half = total.shape[0] // 2
             total, away = total[:half], total[half:].astype(BF16)
         got = exchange(away, distance, size)
-        which = i - (len(order) - 3)
-        if which == -1 or (which == 0 and i == 0):
-            for late in range(ahead, 3):
-                fetched += moments(late, after(first_moment, away), second_moment)
-            got = after(got, *fetched)
-        if which >= 0:
-            pair = fetched[2 * which : 2 * which + 2]
-            news = adam(which, after(kept, away), counts, *operands[which], deltas[which], pair, news)
+        piece = i - (len(order) - 4)
+        ranges = pieces[piece] if piece >= 0 else ()
+        if ranges:
+            news = adam(ranges, after(kept, away), counts, operands, deltas, fetched, news)
         total = total + got.astype(F32)
-        if which >= 0:
+        if ranges:
             total = after(total, *news)
     return (total.astype(BF16), *news)
 

time: 65.9 us -> 65.7 us (level)
  waiting for transfers between devices: 4.14 us -> 2.47 us
  Pallas kernels: 43.7 us -> 44.8 us
    ppermute x12, waiting for transfers between devices: 4.14 us -> 2.47 us  [exchange(): return lax.ppermute(value, 'dp', [(i, i ^ distance) for i in range(size)])]
    pallas_call x3 -> x4, Pallas kernels: 9.73 us -> 11 us  [adam(): pl.pallas_call(functools.partial(adam_kernel, ranges), out_shape=(out, ou...]
  transfers between devices with their start and end apart: 12 -> 12, of which waited for: 4 -> 4; matrix products, arithmetic and copies ran while one was open for 1% -> 1% of each run, Pallas kernels for 30% -> 32%
where the time goes in v5:
time: 65.7 us; the launch traced here: 65.6 us
  Pallas kernels  44.8 us (68%)
  starting transfers between devices  15.9 us (24%)
  waiting for transfers between devices  2.47 us (4%)
  other arithmetic  1.32 us (2%)
  between operations  0.88 us (1%)
    pallas_call x1, Pallas kernels, layer(): pl.pallas_call(functools.partial(layer_kernel, wide, step), out_shape=(pl...  23.8 us
    ppermute x12, starting transfers between devices, exchange(): return lax.ppermute(value, 'dp', [(i, i ^ distance) for i in range(size)])  15.9 us
    pallas_call x4, Pallas kernels, adam(): pl.pallas_call(functools.partial(adam_kernel, ranges), out_shape=(out, ou...  11 us
    pallas_call x2, Pallas kernels, patched(): pl.pallas_call(functools.partial(patch_kernel, which, offset, step), out_...  7.11 us
    pallas_call x1, Pallas kernels, into_vmem(): pl.pallas_call(functools.partial(enter_kernel, per_part, len(whole)), out...  2.95 us
    ppermute x12, waiting for transfers between devices, exchange(): return lax.ppermute(value, 'dp', [(i, i ^ distance) for i in range(size)])  2.47 us
  transfers between devices with their start and end apart: 12, of which 4 were waited for; matrix products, arithmetic and copies ran while one was open for 1% of the time, Pallas kernels for 32%

profile of v5, /device:TPU:0, one launch (start us, length us, event | category | flops | bytes accessed | tf_op | source)
XLA Modules:
  0.0 65.6 jit_solution(10299075829290360250)
XLA Ops:
  0.6 4.1 %collective-permute-start = (bf16[2,8192]{1,0:T(2,128)(2,1)}, bf16[2,8192]{1,0:T(2,128)(2,1)S(1)}, u32[]{:S(2)}, u32[]{:S(2)}) collective-permute-start(bf16[2,8192]{1,0:T(2,128)(2,1)} %refs_0_.1), channel_id=1, source_target_pairs={{0,8},{1,9},{2,10},{3,11},{4,12},{5,13},{6,14},{7,15},{8,0},{9,1},... | collective-permute-start | bytes 98312 | tf_op jit(solution)/shard_map/ppermute | solution.py:436
  4.7 1.5 %collective-permute-start.1 = (bf16[2,8192]{1,0:T(2,128)(2,1)}, bf16[2,8192]{1,0:T(2,128)(2,1)S(1)}, u32[]{:S(2)}, u32[]{:S(2)}) collective-permute-start(bf16[2,8192]{1,0:T(2,128)(2,1)} %refs_1_.1), channel_id=1, source_target_pairs={{0,2},{1,3},{2,0},{3,1},{4,6},{5,7},{6,4},{7,5},{8,10},{9,11},{10,... | collective-permute-start | bytes 98312 | tf_op jit(solution)/shard_map/ppermute | solution.py:436
  6.2 3.0 %enter.1 = (bf16[2,8192]{1,0:T(2,128)(2,1)S(1)}, bf16[2,8192]{1,0:T(2,128)(2,1)S(1)}, s32[3,4,8]{2,1,0:T(4,128)S(4)}, s32[3,8]{1,0:T(4,128)S(4)}, f32[8,4,128,12...) custom-call(bf16[2,8192]{1,0:T(2,128)(2,1)} %refs_0_.1, ...), custom_call_target="tpu_custom_call" | custom-call | tf_op jit(solution)/shard_map/enter/pallas_call | solution.py:117
  9.2 0.0 collective-permute-done
  9.2 0.1 pad_maximum_fusion.4
  9.3 0.0 collective-permute-done.1
  9.3 0.1 pad_maximum_fusion.5
  9.4 0.6 collective-permute-start.3
  10.1 1.9 %collective-permute-start.2 = (bf16[4,8192]{1,0:T(4,128)(2,1)S(1)}, bf16[4,8192]{1,0:T(4,128)(2,1)S(1)}, u32[]{:S(2)}, u32[]{:S(2)}) collective-permute-start(bf16[4,8192]{1,0:T(4,128)(2,1)S(1)} %pad_maximum_fusion.4), channel_id=1, source_target_pairs={{0,4},{1,5},{2,6},{3,7},{4,0},{5,1},{6,2},{7,3},{8,12},{9,13},{10,... | collective-permute-start | bytes 196616 | tf_op jit(solution)/shard_map/ppermute | solution.py:436
  11.9 3.5 %patch.2.gate_0 = bf16[4096,1024]{1,0:T(8,128)(2,1)S(1)} custom-call(s32[3,4,8]{2,1,0:T(4,128)S(4)} %get-tuple-element.99.kept, s32[2,9]{1,0:T(2,128)S(4)} %get-tuple-element.56.begins, s32[2,32]{1,0:T(2,128)S(4)} %get-tuple-element.57.entries, f32[8,4,128,128]{3,2,1,0:T(8,128)S(1)} %get-tuple-element.60.delta.refs_0_, bf16[8192,1024]{1,0:T(8,128)(2,1)} %weight.3), custom_call_target="tpu_custom_call" | custom-call | bytes 8388608 | tf_op jit(solution)/shard_map/patch/pallas_call | solution.py:161
  15.4 0.0 collective-permute-done.3
  15.5 0.1 fusion.3
  15.5 0.2 pad_maximum_fusion.3
  15.7 0.0 collective-permute-done.2
  15.7 0.1 pad_maximum_fusion.2
  15.8 0.8 %collective-permute-start.5 = (bf16[8,8192]{1,0:T(8,128)(2,1)S(1)}, bf16[8,8192]{1,0:T(8,128)(2,1)S(1)}, u32[]{:S(2)}, u32[]{:S(2)}) collective-permute-start(bf16[8,8192]{1,0:T(8,128)(2,1)S(1)} %pad_maximum_fusion.3), channel_id=1, source_target_pairs={{0,4},{1,5},{2,6},{3,7},{4,0},{5,1},{6,2},{7,3},{8,12},{9,13},{10,... | collective-permute-start | bytes 393224 | tf_op jit(solution)/shard_map/ppermute | solution.py:436
  16.6 1.3 %collective-permute-start.4 = (bf16[8,8192]{1,0:T(8,128)(2,1)S(1)}, bf16[8,8192]{1,0:T(8,128)(2,1)S(1)}, u32[]{:S(2)}, u32[]{:S(2)}) collective-permute-start(bf16[8,8192]{1,0:T(8,128)(2,1)S(1)} %pad_maximum_fusion.2), channel_id=1, source_target_pairs={{0,2},{1,3},{2,0},{3,1},{4,6},{5,7},{6,4},{7,5},{8,10},{9,11},{10,... | collective-permute-start | bytes 393224 | tf_op jit(solution)/shard_map/ppermute | solution.py:436
  17.9 3.6 %patch.3.gate_1 = bf16[4096,1024]{1,0:T(8,128)(2,1)S(1)} custom-call(s32[3,4,8]{2,1,0:T(4,128)S(4)} %get-tuple-element.99.kept, s32[2,9]{1,0:T(2,128)S(4)} %get-tuple-element.56.begins, s32[2,32]{1,0:T(2,128)S(4)} %get-tuple-element.57.entries, f32[8,4,128,128]{3,2,1,0:T(8,128)S(1)} %get-tuple-element.60.delta.refs_0_, bf16[8192,1024]{1,0:T(8,128)(2,1)} %weight.3), custom_call_target="tpu_custom_call" | custom-call | bytes 8388608 | tf_op jit(solution)/shard_map/patch/pallas_call | solution.py:161
  21.5 0.0 collective-permute-done.5
  21.6 0.2 pad_maximum_fusion.1.cotangent_0
  21.8 0.0 collective-permute-done.4
  21.8 0.1 collective-permute-start.6
  21.9 0.5 collective-permute-start.7
  22.4 1.0 %collective-permute-done.6.tokens_1 = bf16[16,8192]{1,0:T(8,128)(2,1)S(1)} collective-permute-done((bf16[16,8192]{1,0:T(8,128)(2,1)S(1)}, bf16[16,8192]{1,0:T(8,128)(2,1)S(1)}, u32[]{:S(2)}, u32[]{:S(2)}) %collective-permute-start.6) | collective-permute-done | bytes 262176 | tf_op jit(solution)/shard_map/ppermute | solution.py:436
  23.4 0.4 collective-permute-done.7.cotangent_1
  23.8 23.8 %layer.1 = (f32[16,8192]{1,0:T(8,128)S(1)}, bf16[16,8192]{1,0:T(8,128)(2,1)S(1)}, bf16[32,8192]{1,0:T(8,128)(2,1)S(1)}, bf16[32,8192]{1,0:T(8,128)(2,1)S(1)}, bf...) custom-call(s32[3,4,8]{2,1,0:T(4,128)S(4)} %get-tuple-element.99.kep, ...), custom_call_target="tpu_custom_call" | custom-call | flops 2684354560 | bytes 83886080 | tf_op jit(solution)/shard_map/layer/pallas_call | solution.py:327
  47.5 0.4 collective-permute-start.8
  48.0 1.6 %adam.4 = (f32[3,8,4,128,128]{4,3,2,1,0:T(8,128)}, f32[3,8,4,128,128]{4,3,2,1,0:T(8,128)}, f32[3,8,4,128,128]{4,3,2,1,0:T(8,128)}) custom-call(s32[3,4,8]{2,1,0:T(4,128)S(4)} %get-tuple-element.99.kept, s32[3,8]{1,0:T(4,128)S(4)} %get-tuple-element.55.counts, bf16[32,1024]{1,0:T(8,128)(2,1)S(1)} %get-tuple-element.74.hidden, ...), custom_call_target="tpu_custom_call" | custom-call | bytes 1572864 | tf_op jit(solution)/shard_map/adam/pallas_call | solution.py:411
  49.5 0.0 collective-permute-done.8
  49.6 1.1 %collective-permute-start.9 = (bf16[8,8192]{1,0:T(8,128)(2,1)S(1)}, bf16[8,8192]{1,0:T(8,128)(2,1)S(1)}, u32[]{:S(2)}, u32[]{:S(2)}) collective-permute-start(bf16[8,8192]{1,0:T(8,128)(2,1)S(1)} %slice.72), channel_id=1, source_target_pairs={{0,2},{1,3},{2,0},{3,1},{4,6},{5,7},{6,4},{7,5},{8,10},{9,11},{10,... | collective-permute-start | bytes 393224 | tf_op jit(solution)/shard_map/ppermute | solution.py:436
  50.7 3.8 %adam.5 = (f32[3,8,4,128,128]{4,3,2,1,0:T(8,128)}, f32[3,8,4,128,128]{4,3,2,1,0:T(8,128)}, f32[3,8,4,128,128]{4,3,2,1,0:T(8,128)}) custom-call(s32[3,4,8]{2,1,0:T(4,128)S(4)} %get-tuple-element.99.kept, s32[3,8]{1,0:T(4,128)S(4)} %get-tuple-element.55.counts, ...), custom_call_target="tpu_custom_call", output_to_operand_aliasing={{0}: (13, {}), {1}: (14, {}), {2}: (15, {})} | custom-call | bytes 7864320 | tf_op jit(solution)/shard_map/adam/pallas_call | solution.py:411
  54.5 0.7 %collective-permute-done.9 = bf16[8,8192]{1,0:T(8,128)(2,1)S(1)} collective-permute-done((bf16[8,8192]{1,0:T(8,128)(2,1)S(1)}, bf16[8,8192]{1,0:T(8,128)(2,1)S(1)}, u32[]{:S(2)}, u32[]{:S(2)}) %collective-permute-start.9) | collective-permute-done | bytes 131104 | tf_op jit(solution)/shard_map/ppermute | solution.py:436
  55.3 1.8 %collective-permute-start.10 = (bf16[4,8192]{1,0:T(4,128)(2,1)S(1)}, bf16[4,8192]{1,0:T(4,128)(2,1)S(1)}, u32[]{:S(2)}, u32[]{:S(2)}) collective-permute-start(bf16[4,8192]{1,0:T(4,128)(2,1)S(1)} %slice.73), channel_id=1, source_target_pairs={{0,4},{1,5},{2,6},{3,7},{4,0},{5,1},{6,2},{7,3},{8,12},{9,13},{10,... | collective-permute-start | bytes 196616 | tf_op jit(solution)/shard_map/ppermute | solution.py:436
  57.1 2.8 %adam.6 = (f32[3,8,4,128,128]{4,3,2,1,0:T(8,128)}, f32[3,8,4,128,128]{4,3,2,1,0:T(8,128)}, f32[3,8,4,128,128]{4,3,2,1,0:T(8,128)}) custom-call(s32[3,4,8]{2,1,0:T(4,128)S(4)} %get-tuple-element.99.kept, s32[3,8]{1,0:T(4,128)S(4)} %get-tuple-element.55.counts, ...), custom_call_target="tpu_custom_call", output_to_operand_aliasing={{0}: (10, {}), {1}: (11, {}), {2}: (12, {})} | custom-call | bytes 4718592 | tf_op jit(solution)/shard_map/adam/pallas_call | solution.py:411
  60.0 0.0 collective-permute-done.10
  60.1 1.8 %collective-permute-start.11 = (bf16[2,8192]{1,0:T(2,128)(2,1)S(1)}, bf16[2,8192]{1,0:T(2,128)(2,1)S(1)}, u32[]{:S(2)}, u32[]{:S(2)}) collective-permute-start(bf16[2,8192]{1,0:T(2,128)(2,1)S(1)} %slice.74), channel_id=1, source_target_pairs={{0,8},{1,9},{2,10},{3,11},{4,12},{5,13},{6,14},{7,15},{8,0},{9,1},... | collective-permute-start | bytes 98312 | tf_op jit(solution)/shard_map/ppermute | solution.py:436
  61.8 2.8 %adam.7 = (f32[3,8,4,128,128]{4,3,2,1,0:T(8,128)}, f32[3,8,4,128,128]{4,3,2,1,0:T(8,128)}, f32[3,8,4,128,128]{4,3,2,1,0:T(8,128)}) custom-call(s32[3,4,8]{2,1,0:T(4,128)S(4)} %get-tuple-element.99.kept, s32[3,8]{1,0:T(4,128)S(4)} %get-tuple-element.55.counts, ...), custom_call_target="tpu_custom_call", output_to_operand_aliasing={{0}: (10, {}), {1}: (11, {}), {2}: (12, {})} | custom-call | bytes 4718592 | tf_op jit(solution)/shard_map/adam/pallas_call | solution.py:411
  64.6 0.3 collective-permute-done.11
  64.9 0.7 convert_add_fusion.3
  (10 shorter events, 0.4 us)
Async XLA Ops:
  0.6 8.6 %collective-permute-start = (bf16[2,8192]{1,0:T(2,128)(2,1)}, bf16[2,8192]{1,0:T(2,128)(2,1)S(1)}, u32[]{:S(2)}, u32[]{:S(2)}) collective-permute-start(bf16[2,8192]{1,0:T(2,128)(2,1)} %refs_0_.1), channel_id=1, source_target_pairs={{0,8},{1,9},{2,10},{3,11},{4,12},{5,13},{6,14},{7,15},{8,0},{9,1},... | collective-permute-start | bytes 98312 | tf_op jit(solution)/shard_map/ppermute | solution.py:436
  4.7 4.5 %collective-permute-start.1 = (bf16[2,8192]{1,0:T(2,128)(2,1)}, bf16[2,8192]{1,0:T(2,128)(2,1)S(1)}, u32[]{:S(2)}, u32[]{:S(2)}) collective-permute-start(bf16[2,8192]{1,0:T(2,128)(2,1)} %refs_1_.1), channel_id=1, source_target_pairs={{0,2},{1,3},{2,0},{3,1},{4,6},{5,7},{6,4},{7,5},{8,10},{9,11},{10,... | collective-permute-start | bytes 98312 | tf_op jit(solution)/shard_map/ppermute | solution.py:436
  9.4 6.1 %collective-permute-start.3 = (bf16[4,8192]{1,0:T(4,128)(2,1)S(1)}, bf16[4,8192]{1,0:T(4,128)(2,1)S(1)}, u32[]{:S(2)}, u32[]{:S(2)}) collective-permute-start(bf16[4,8192]{1,0:T(4,128)(2,1)S(1)} %pad_maximum_fusion.5), channel_id=1, source_target_pairs={{0,8},{1,9},{2,10},{3,11},{4,12},{5,13},{6,14},{7,15},{8,0},{9,1},... | collective-permute-start | bytes 196616 | tf_op jit(solution)/shard_map/ppermute | solution.py:436
  10.1 5.6 %collective-permute-start.2 = (bf16[4,8192]{1,0:T(4,128)(2,1)S(1)}, bf16[4,8192]{1,0:T(4,128)(2,1)S(1)}, u32[]{:S(2)}, u32[]{:S(2)}) collective-permute-start(bf16[4,8192]{1,0:T(4,128)(2,1)S(1)} %pad_maximum_fusion.4), channel_id=1, source_target_pairs={{0,4},{1,5},{2,6},{3,7},{4,0},{5,1},{6,2},{7,3},{8,12},{9,13},{10,... | collective-permute-start | bytes 196616 | tf_op jit(solution)/shard_map/ppermute | solution.py:436
  15.8 5.8 %collective-permute-start.5 = (bf16[8,8192]{1,0:T(8,128)(2,1)S(1)}, bf16[8,8192]{1,0:T(8,128)(2,1)S(1)}, u32[]{:S(2)}, u32[]{:S(2)}) collective-permute-start(bf16[8,8192]{1,0:T(8,128)(2,1)S(1)} %pad_maximum_fusion.3), channel_id=1, source_target_pairs={{0,4},{1,5},{2,6},{3,7},{4,0},{5,1},{6,2},{7,3},{8,12},{9,13},{10,... | collective-permute-start | bytes 393224 | tf_op jit(solution)/shard_map/ppermute | solution.py:436
  16.6 5.2 %collective-permute-start.4 = (bf16[8,8192]{1,0:T(8,128)(2,1)S(1)}, bf16[8,8192]{1,0:T(8,128)(2,1)S(1)}, u32[]{:S(2)}, u32[]{:S(2)}) collective-permute-start(bf16[8,8192]{1,0:T(8,128)(2,1)S(1)} %pad_maximum_fusion.2), channel_id=1, source_target_pairs={{0,2},{1,3},{2,0},{3,1},{4,6},{5,7},{6,4},{7,5},{8,10},{9,11},{10,... | collective-permute-start | bytes 393224 | tf_op jit(solution)/shard_map/ppermute | solution.py:436
  21.8 1.6 %collective-permute-start.6 = (bf16[16,8192]{1,0:T(8,128)(2,1)S(1)}, bf16[16,8192]{1,0:T(8,128)(2,1)S(1)}, u32[]{:S(2)}, u32[]{:S(2)}) collective-permute-start(bf16[16,8192]{1,0:T(8,128)(2,1)S(1)} %pad_maximum_fusion.tokens_0), channel_id=1, source_target_pairs={{0,1},{1,0},{2,3},{3,2},{4,5},{5,4},{6,7},{7,6},{8,9},{9,8},{10,11... | collective-permute-start | bytes 786440 | tf_op jit(solution)/shard_map/ppermute | solution.py:436
  21.9 1.9 %collective-permute-start.7 = (bf16[16,8192]{1,0:T(8,128)(2,1)S(1)}, bf16[16,8192]{1,0:T(8,128)(2,1)S(1)}, u32[]{:S(2)}, u32[]{:S(2)}) collective-permute-start(bf16[16,8192]{1,0:T(8,128)(2,1)S(1)} %pad_maximum_fusion.1.cotangent_0), channel_id=1, source_target_pairs={{0,1},{1,0},{2,3},{3,2},{4,5},{5,4},{6,7},{7,6},{8,9},{9,8},{10,11... | collective-permute-start | bytes 786440 | tf_op jit(solution)/shard_map/ppermute | solution.py:436
  47.5 2.0 %collective-permute-start.8 = (bf16[16,8192]{1,0:T(8,128)(2,1)S(1)}, bf16[16,8192]{1,0:T(8,128)(2,1)S(1)}, u32[]{:S(2)}, u32[]{:S(2)}) collective-permute-start(bf16[16,8192]{1,0:T(8,128)(2,1)S(1)} %get-tuple-element.72), channel_id=1, source_target_pairs={{0,1},{1,0},{2,3},{3,2},{4,5},{5,4},{6,7},{7,6},{8,9},{9,8},{10,11... | collective-permute-start | bytes 786440 | tf_op jit(solution)/shard_map/ppermute | solution.py:436
  49.6 5.6 %collective-permute-start.9 = (bf16[8,8192]{1,0:T(8,128)(2,1)S(1)}, bf16[8,8192]{1,0:T(8,128)(2,1)S(1)}, u32[]{:S(2)}, u32[]{:S(2)}) collective-permute-start(bf16[8,8192]{1,0:T(8,128)(2,1)S(1)} %slice.72), channel_id=1, source_target_pairs={{0,2},{1,3},{2,0},{3,1},{4,6},{5,7},{6,4},{7,5},{8,10},{9,11},{10,... | collective-permute-start | bytes 393224 | tf_op jit(solution)/shard_map/ppermute | solution.py:436
  55.3 4.6 %collective-permute-start.10 = (bf16[4,8192]{1,0:T(4,128)(2,1)S(1)}, bf16[4,8192]{1,0:T(4,128)(2,1)S(1)}, u32[]{:S(2)}, u32[]{:S(2)}) collective-permute-start(bf16[4,8192]{1,0:T(4,128)(2,1)S(1)} %slice.73), channel_id=1, source_target_pairs={{0,4},{1,5},{2,6},{3,7},{4,0},{5,1},{6,2},{7,3},{8,12},{9,13},{10,... | collective-permute-start | bytes 196616 | tf_op jit(solution)/shard_map/ppermute | solution.py:436
  60.1 4.9 %collective-permute-start.11 = (bf16[2,8192]{1,0:T(2,128)(2,1)S(1)}, bf16[2,8192]{1,0:T(2,128)(2,1)S(1)}, u32[]{:S(2)}, u32[]{:S(2)}) collective-permute-start(bf16[2,8192]{1,0:T(2,128)(2,1)S(1)} %slice.74), channel_id=1, source_target_pairs={{0,8},{1,9},{2,10},{3,11},{4,12},{5,13},{6,14},{7,15},{8,0},{9,1},... | collective-permute-start | bytes 98312 | tf_op jit(solution)/shard_map/ppermute | solution.py:436
